TPU v7x, 32 devices: a whole 2x2x4 slice. The times are simulated.
32 devices in a mesh: seq: 8 (over z, x), tp: 4 (over y, core).
Axes of the slice: x: 2, y: 2, z: 4, core: 2. Of those that a mesh axis runs over, the one named last changes fastest.
Arguments:
- state: bfloat16 [2304, 3072], P('seq', 'tp'), may hold values from -40 to 40
- latent: float32 [1152, 64], P('seq'), may hold values from -6 to 6
- w_mod: bfloat16 [3072, 9216], P('tp', 'seq'), may hold values from -0.109375 to 0.109375
- w_qkv: bfloat16 [3072, 3, 1536], P(None, None, 'tp'), may hold values from -1 to 1
- w_mlp_in: bfloat16 [3072, 6144], P('seq', 'tp'), may hold values from -0.109375 to 0.109375
- q_gain: float32 [12, 128], P('tp'), may hold values from 1.4 to 6.6
- k_gain: float32 [12, 128], P('tp'), may hold values from 1.4 to 6.6
- w_out: bfloat16 [1536, 3072], P('tp'), may hold values from -0.15625 to 0.15625
- w_mlp_down: bfloat16 [3072, 6144], P('seq', 'tp'), may hold values from -0.078125 to 0.078125
- w_final: bfloat16 [3072, 64], P('tp'), may hold values from -0.109375 to 0.109375
- text_len: int32 [2, 2], replicated, may hold values from 64 to 512, as said below
- rope_ids: int32 [3, 2304], P(None, 'seq'), may hold values from 0 to 126, as said below
- guidance: int32 [2], replicated, may hold values from 2 to 12
- step_index: int32 [2], replicated, may hold values from 0 to 27
Outputs:
- new_state: bfloat16 [2304, 3072], P('seq', 'tp')
- next_latent: float32 [1152, 64], P('seq')
- state_norm: float32 [2], replicated
- top_score: float32 [2], replicated
Inputs may be any that keep to these rules, and one draw needn't show every extreme that they name: `text_len`: one of the entries equals 512, a different one from draw to draw. `rope_ids`: text positions have ids (0, 0, 0); image position p >= 512 has (frame, row offset + (p - 512) // 64, column offset + (p - 512) % 64), with a frame of 0 or 1 and offsets of 0 to 63 for each request, the same in both halves; one request has row offset 63 and one has column offset 63.
All inputs are finite; a program needn't handle non-finite values.
Results may differ from a plain program's by a relative error of at most 0.008.
Values may be sent and summed in bfloat16 or wider, within the bound.
A program may use at most 192 MiB of HBM per device.

v0:
```python
import math

import jax
import jax.numpy as jnp
from jax import lax
from jax.sharding import PartitionSpec as P

D = 3072
HD = 128
REQ = 2
TOK_DEV = 288
TXT = 512
STEPS = 28


TIME_SHIFT = 1.15
ROPE_THETA = 10000.0
NORM_EPS = 1e-06
MASKED_SCORE = -1e30


def partner(value, axis, apart):
    return lax.ppermute(value, axis, [(i, i ^ 1 << apart) for i in range(lax.axis_size(axis))])


def merged(value, axis, join):
    pieces = jax.tree.map(lambda part: lax.all_gather(part, axis), value)
    head = jax.tree.map(lambda part: part[0], pieces)
    tail = jax.tree.map(lambda part: part[1:], pieces)
    total, _ = lax.scan(lambda total, section: (join(total, section), None), head, tail)
    return total


def sigma_of(step_count):
    fraction = 1.0 - step_count.astype(jnp.float32) / STEPS
    boosted = math.exp(TIME_SHIFT) * fraction
    return boosted / (boosted + 1.0 - fraction)


def time_embedding(sigma_vals):
    half_width = D // 2
    frequency = jnp.exp(-math.log(10000.0) * jnp.arange(half_width, dtype=jnp.float32) / half_width)
    phases = 1000.0 * sigma_vals[:, None] * frequency[None, :]
    return jnp.concatenate([jnp.cos(phases), jnp.sin(phases)], axis=1)


def layer_norm(rows):
    center = jnp.mean(rows, axis=-1, keepdims=True)
    spread = jnp.mean(jnp.square(rows - center), axis=-1, keepdims=True)
    return (rows - center) * lax.rsqrt(spread + NORM_EPS)


def rms_norm(rows):
    return rows * lax.rsqrt(jnp.mean(jnp.square(rows), axis=-1, keepdims=True) + NORM_EPS)


def rope_angles(id_rows):
    pieces = []
    for component, width in enumerate((HD // 8, 7 * HD // 16, 7 * HD // 16)):
        index_vec = jnp.arange(width // 2, dtype=jnp.float32)
        omega = jnp.exp(-math.log(ROPE_THETA) * 2.0 * index_vec / width)
        pieces.append(id_rows[component].astype(jnp.float32)[:, None] * omega[None, :])
    return jnp.concatenate(pieces, axis=1)


def rotate(rows, angles):
    count, heads_here, size = rows.shape
    paired = rows.reshape(count, heads_here, size // 2, 2)
    cosine = jnp.cos(angles)[:, None, :]
    sine = jnp.sin(angles)[:, None, :]
    first = paired[..., 0]
    second = paired[..., 1]
    turned = jnp.stack([first * cosine - second * sine, first * sine + second * cosine], axis=-1)
    return turned.reshape(count, heads_here, size)


def combine_stats(first_pair, second_pair):
    return (first_pair[0] + second_pair[0], jnp.maximum(first_pair[1], second_pair[1]))


def down_product(hidden_rows, weight_rows):
    return lax.dot_general(
        hidden_rows, weight_rows, (((1,), (1,)), ((), ())), preferred_element_type=jnp.float32
    )


def body(
    state,
    latent,
    w_mod,
    w_qkv,
    w_mlp_in,
    q_gain,
    k_gain,
    w_out,
    w_mlp_down,
    w_final,
    text_len,
    rope_ids,
    guidance,
    step_index,
):
    blocks = lax.axis_size("seq") // (2 * REQ)
    seq_len = TOK_DEV * blocks
    seq_index = lax.axis_index("seq")
    tp_index = lax.axis_index("tp")
    request = seq_index // (2 * blocks)
    block = seq_index // 2 % blocks
    guided_half = seq_index % 2
    width_tp = state.shape[1]
    request_pick = jnp.arange(REQ, dtype=jnp.int32) == request
    sigma_now = sigma_of(step_index)
    step_size = sigma_of(step_index + 1) - sigma_now
    time_vec = jax.nn.silu(time_embedding(sigma_now)).astype(jnp.bfloat16)
    time_rows = lax.dynamic_slice_in_dim(time_vec, tp_index * width_tp, width_tp, 1)
    partial_mod = jnp.dot(time_rows, w_mod, preferred_element_type=jnp.float32)
    summed_mod = lax.psum(partial_mod, "tp")
    modulation = lax.all_gather(summed_mod, "seq", axis=1, tiled=True)
    own_mod = jnp.sum(jnp.where(request_pick[:, None], modulation, 0.0), axis=0)
    shift_vec = own_mod[:D]
    scale_vec = own_mod[D : 2 * D]
    gate_vec = lax.dynamic_slice_in_dim(own_mod[2 * D :], tp_index * width_tp, width_tp, 0)
    full_rows = lax.all_gather(state, "tp", axis=1, tiled=True)
    modded = ((1.0 + scale_vec) * layer_norm(full_rows.astype(jnp.float32)) + shift_vec).astype(
        jnp.bfloat16
    )
    heads_here = w_qkv.shape[2] // HD
    projected = jnp.dot(
        modded, w_qkv.reshape(D, 3 * heads_here * HD), preferred_element_type=jnp.float32
    )
    projected = projected.reshape(TOK_DEV, 3, heads_here, HD)
    mlp_pre = jnp.dot(
        modded,
        lax.all_gather(w_mlp_in, "seq", axis=0, tiled=True),
        preferred_element_type=jnp.float32,
    )
    mlp_hidden = jax.nn.gelu(mlp_pre, approximate=True).astype(jnp.bfloat16)
    mlp_term = down_product(mlp_hidden, lax.all_gather(w_mlp_down, "seq", axis=0, tiled=True))
    angles = rope_angles(rope_ids)
    queries = rotate(rms_norm(projected[:, 0]) * q_gain[None], angles).astype(jnp.bfloat16)
    key_rows = rotate(rms_norm(projected[:, 1]) * k_gain[None], angles).astype(jnp.bfloat16)
    value_rows = projected[:, 2].astype(jnp.bfloat16)
    positions = block * TOK_DEV + jnp.arange(TOK_DEV, dtype=jnp.int32)
    bit_count = blocks.bit_length() - 1
    levels = range(bit_count)
    for level in levels:
        other_keys, other_values = partner((key_rows, value_rows), "seq", level + 1)
        flip_bit = block // 2**level % 2
        other_positions = positions + (1 - 2 * flip_bit) * 2**level * TOK_DEV
        key_rows = jnp.concatenate([key_rows, other_keys], axis=0)
        value_rows = jnp.concatenate([value_rows, other_values], axis=0)
        positions = jnp.concatenate([positions, other_positions], axis=0)
    flat_len = text_len.reshape(2 * REQ)
    own_len = jnp.sum(
        jnp.where(jnp.arange(2 * REQ, dtype=jnp.int32) == request * 2 + guided_half, flat_len, 0)
    )
    live = (positions >= TXT) | (positions < own_len)
    scores = jnp.einsum("qhd,khd->hqk", queries, key_rows, preferred_element_type=jnp.float32) * (
        1.0 / math.sqrt(HD)
    )
    scores = jnp.where(live[None, None, :], scores, MASKED_SCORE)
    row_max = jnp.max(scores, axis=2, keepdims=True)
    top_local = jnp.max(row_max)
    weights = jnp.exp(scores - row_max)
    weights = (weights / jnp.sum(weights, axis=2, keepdims=True)).astype(jnp.bfloat16)
    attended = jnp.einsum("hqk,khd->qhd", weights, value_rows, preferred_element_type=jnp.float32)
    attended = attended.astype(jnp.bfloat16).reshape(TOK_DEV, heads_here * HD)
    term = jnp.dot(attended, w_out, preferred_element_type=jnp.float32) + mlp_term
    update = lax.psum_scatter(
        term.astype(jnp.bfloat16), "tp", scatter_dimension=1, tiled=True
    ).astype(jnp.float32)
    new_state = (state.astype(jnp.float32) + gate_vec * update).astype(jnp.bfloat16)
    state_values = new_state.astype(jnp.float32)
    row_total, row_squares = lax.psum(
        (jnp.sum(state_values, axis=1), jnp.sum(state_values * state_values, axis=1)), "tp"
    )
    row_mean = (row_total / D)[:, None]
    row_var = (row_squares / D)[:, None] - row_mean * row_mean
    normed_out = ((state_values - row_mean) * lax.rsqrt(row_var + NORM_EPS)).astype(jnp.bfloat16)
    velocity_part = jnp.dot(normed_out, w_final, preferred_element_type=jnp.float32)
    velocity = lax.psum(velocity_part.astype(jnp.bfloat16), "tp").astype(jnp.float32)
    half_rows = TOK_DEV // 2
    keep_part = lax.dynamic_slice_in_dim(velocity, guided_half * half_rows, half_rows, 0)
    give_part = lax.dynamic_slice_in_dim(velocity, (1 - guided_half) * half_rows, half_rows, 0)
    taken_part = partner(give_part.astype(jnp.bfloat16), "seq", 0).astype(give_part.dtype)
    cond_part = jnp.where(guided_half == 0, keep_part, taken_part)
    uncond_part = jnp.where(guided_half == 0, taken_part, keep_part)
    guide_scale = jnp.sum(jnp.where(request_pick, guidance, 0)).astype(jnp.float32) / 2.0
    own_step = jnp.sum(jnp.where(request_pick, step_size, 0.0))
    next_latent = latent + own_step * (uncond_part + guide_scale * (cond_part - uncond_part))
    square_vec = jnp.where(request_pick, jnp.sum(state_values * state_values), 0.0)
    peak_vec = jnp.where(request_pick, top_local, MASKED_SCORE)
    square_total, top_score = merged((square_vec, peak_vec), ("seq", "tp"), combine_stats)
    state_norm = jnp.sqrt(square_total / (2.0 * seq_len * D))
    return (new_state, next_latent, state_norm, top_score)


def solution(mesh):
    in_specs = (
        P("seq", "tp"),
        P("seq", None),
        P("tp", "seq"),
        P(None, None, "tp"),
        P("seq", "tp"),
        P("tp", None),
        P("tp", None),
        P("tp", None),
        P("seq", "tp"),
        P("tp", None),
        P(),
        P(None, "seq"),
        P(),
        P(),
    )
    out_specs = (P("seq", "tp"), P("seq", None), P(), P())
    return jax.shard_map(body, mesh=mesh, in_specs=in_specs, out_specs=out_specs, check_vma=False)
```

profile of v0, /device:TPU:0, one launch (start us, length us, event | category | flops | bytes accessed | tf_op | source)
XLA Modules:
  0.0 447.0 jit_solution(16407234253631110188)
XLA Ops:
  9.6 10.4 %copy.33 = bf16[3072,3,384]{0,2,1:T(8,128)(2,1)} copy(bf16[3072,3,384]{2,0,1:T(8,128)(2,1)} %param.19) | data formatting | bytes 14155776 | tf_op args[3]
  22.5 1.8 fusion.64
  24.3 9.1 %psum.28 = f32[2,1152]{1,0:T(2,128)S(1)} all-reduce(f32[2,1152]{1,0:T(2,128)S(1)} %fusion.64), channel_id=1, replica_groups=mesh['seq'=8,'tp'=4] {'tp'}, use_global_device_ids=true, to_apply=%region_0.1 | all-reduce | flops 2304 | bytes 18432 | tf_op jit(solution)/shard_map/psum | solution.py:117
  33.3 31.3 %all_gather.20 = f32[2,9216]{1,0:T(2,128)S(1)} all-gather(f32[2,1152]{1,0:T(2,128)S(1)} %psum.28), channel_id=1, replica_groups=mesh['seq'=8,'tp'=4] {'seq'}, dimensions={1}, use_global_device_ids=true | all-gather | bytes 82944 | tf_op jit(solution)/shard_map/all_gather | solution.py:118
  68.7 1.9 convert_reduce_fusion
  71.4 5.0 %fusion.20 = f32[288,3,3,128]{3,0,2,1:T(8,128)S(1)} fusion(bf16[3,3,128,3072]{3,2,1,0:T(8,128)(2,1)} %bitcast.62, bf16[288,3072]{1,0:T(8,128)(2,1)S(1)} %copy-done.1, f32[3072]{0:T(1024)S(1)} %get-tuple-element.85, f32[288]{0:T(512)S(1)} %add_rsqrt_fusion.3, f32[288]{0:T(512)S(1)} %broadcast_multiply_fusion.4, f32[3072]{0:T(1024)S(1)} %get-tuple-element.86), kind=kOutput, calls=%fused_computation.29 | convolution fusion | flops 2043740160 | bytes 10201344 | tf_op jit(solution)/shard_map/dot_general | solution.py:128
  78.2 2.1 copy.34
  80.3 1.4 squeeze.27
  84.2 1.8 subtract_convert_fusion
  89.2 2.1 collective-permute-start
  91.3 2.8 collective-permute-done.1
  94.1 2.3 fusion.87
  97.2 2.2 fusion.24
  99.3 77.2 %all-gather.10.cloned.1.call-done = bf16[3072,1536]{1,0:T(8,128)(2,1)} async-done(((bf16[384,1536]{1,0:T(8,128)(2,1)}), bf16[3072,1536]{1,0:T(8,128)(2,1)}) %all-gather.10.cloned.1.call-update) | async-done | bytes 9437200 | tf_op jit(solution)/shard_map/all_gather | solution.py:138
  176.6 138.5 %all-gather.8.cloned.1.call-done = bf16[3072,1536]{1,0:T(8,128)(2,1)} async-done(((bf16[384,1536]{1,0:T(8,128)(2,1)}), bf16[3072,1536]{1,0:T(8,128)(2,1)}) %all-gather.8.cloned.1.call-update) | async-done | bytes 9437200 | tf_op jit(solution)/shard_map/all_gather | solution.py:134
  315.0 14.6 %fusion.32 = f32[288,3072]{1,0:T(8,128)} fusion(bf16[3072,1536]{1,0:T(8,128)(2,1)} %all-gather.10.cloned.1.call-done, bf16[3072,1536]{1,0:T(8,128)(2,1)} %all-gather.8.cloned.1.call-done, bf16[288,3072]{1,0:T(8,128)(2,1)} %all-gather.6.cloned.1.call-done, f32[3072]{0:T(1024)S(1)} %copy-done.10, f32[288]{0:T(512)S(1)} %copy-done.19, f32[288]{0:T(512)S(1)} %copy-done.14, ...), kind=kOutput, calls=%fused_computation.46 | convolution fusion | flops 5445107712 | bytes 24209664 | tf_op jit(solution)/shard_map/dot_general | solution.py:82
  329.6 4.3 fusion.7
  338.2 38.4 %all-gather.1 = f32[32,1,2]{2,1,0:T(1,128)S(1)} all-gather(f32[1,1,2]{2,1,0:T(1,128)S(1)} %fusion.70), channel_id=1, replica_groups=mesh['seq'=8,'tp'=4] {'seq','tp'}, dimensions={0}, use_global_device_ids=true | all-gather | bytes 264 | tf_op jit(solution)/shard_map/all_gather | solution.py:27
  376.8 2.0 fusion.28
  379.5 36.4 %all-gather = f32[32,1,2]{2,1,0:T(1,128)S(1)} all-gather(f32[1,1,2]{2,1,0:T(1,128)S(1)} %fusion.69), channel_id=1, replica_groups=mesh['seq'=8,'tp'=4] {'seq','tp'}, dimensions={0}, use_global_device_ids=true | all-gather | bytes 264 | tf_op jit(solution)/shard_map/all_gather | solution.py:27
  415.9 7.3 %all-reduce = (f32[288]{0:T(512)S(1)}, f32[288]{0:T(512)S(1)}) all-reduce(f32[288]{0:T(512)S(1)} %get-tuple-element.52, f32[288]{0:T(512)S(1)} %get-tuple-element.53), channel_id=1, replica_groups=mesh['seq'=8,'tp'=4] {'tp'}, use_global_device_ids=true, to_apply=%region_14.15 | all-reduce | flops 576 | bytes 4608 | tf_op jit(solution)/shard_map/psum | solution.py:174
  424.4 10.6 %psum.31 = bf16[288,64]{0,1:T(8,128)(2,1)S(1)} all-reduce(bf16[288,64]{0,1:T(8,128)(2,1)S(1)} %convolution_convert_fusion.1), channel_id=1, replica_groups=mesh['seq'=8,'tp'=4] {'tp'}, use_global_device_ids=true, to_apply=%region_15.16 | all-reduce | flops 18432 | bytes 73728 | tf_op jit(solution)/shard_map/psum | solution.py:181
  437.0 2.1 collective-permute-done.2
  439.1 1.4 fusion.59
  (150 shorter events, 25.9 us)
Async XLA Ops:
  7.2 322.4 %copy-start = (bf16[384,3072]{1,0:T(8,128)(2,1)S(1)}, bf16[384,3072]{1,0:T(8,128)(2,1)}, u32[]{:S(2)}) copy-start(bf16[384,3072]{1,0:T(8,128)(2,1)} %param.23) | copy-start | bytes 7077892
  7.2 61.5 %all-gather.6.cloned.1.call-start = ((), (), s32[]{:S(2)}) async-start(), calls=%async_computation.1 | async-start | bytes 2211840 | tf_op jit(solution)/shard_map/all_gather | solution.py:123
  7.9 168.6 %all-gather.10.cloned.1.call-start = ((), (), s32[]{:S(2)}) async-start(), calls=%async_computation.3 | async-start | bytes 10616832 | tf_op jit(solution)/shard_map/all_gather | solution.py:138
  8.7 306.4 %all-gather.8.cloned.1.call-start = ((), (), s32[]{:S(2)}) async-start(), calls=%async_computation.2 | async-start | bytes 10616832 | tf_op jit(solution)/shard_map/all_gather | solution.py:134
  9.4 367.4 %reduce-scatter.2.cloned.1.call-start = ((), (), s32[]{:S(2)}) async-start(), calls=%async_computation.4 | async-start | bytes 2211840 | tf_op jit(solution)/shard_map/reduce_scatter | solution.py:169
  9.5 10.4 %copy-start.16 = (f32[3,128]{1,0:T(4,128)S(1)}, f32[3,128]{1,0:T(4,128)}, u32[]{:S(2)}) copy-start(f32[3,128]{1,0:T(4,128)} %param.22) | copy-start | bytes 4612
  9.5 11.2 %copy-start.17 = (f32[3,128]{1,0:T(4,128)S(1)}, f32[3,128]{1,0:T(4,128)}, u32[]{:S(2)}) copy-start(f32[3,128]{1,0:T(4,128)} %param.21) | copy-start | bytes 4612
  9.5 12.0 %copy-start.22 = (s32[2]{0:T(128)S(1)}, s32[2]{0:T(128)}, u32[]{:S(2)}) copy-start(s32[2]{0:T(128)} %param.29) | copy-start | bytes 28
  9.5 55.2 %copy-start.20 = (s32[2,2]{1,0:T(2,128)S(1)}, s32[2,2]{1,0:T(2,128)}, u32[]{:S(2)}) copy-start(s32[2,2]{1,0:T(2,128)} %param.26) | copy-start | bytes 52
  9.6 57.1 %copy-start.15 = (s32[3,288]{1,0:T(4,128)S(1)}, s32[3,288]{1,0:T(4,128)}, u32[]{:S(2)}) copy-start(s32[3,288]{1,0:T(4,128)} %param.27) | copy-start | bytes 10372
  68.7 7.7 %copy-start.9 = (f32[3072]{0:T(1024)}, f32[3072]{0:T(1024)S(1)}, u32[]{:S(2)}) copy-start(f32[3072]{0:T(1024)S(1)} %get-tuple-element.85) | copy-start | bytes 36868
  68.7 7.7 %copy-start.11 = (f32[3072]{0:T(1024)}, f32[3072]{0:T(1024)S(1)}, u32[]{:S(2)}) copy-start(f32[3072]{0:T(1024)S(1)} %get-tuple-element.86) | copy-start | bytes 36868
  86.0 8.1 %copy-start.21 = (pred[576]{0:T(1024)(128)(4,1)S(1)}, pred[576]{0:T(1024)(128)(4,1)}, u32[]{:S(2)}) copy-start(pred[576]{0:T(1024)(128)(4,1)} %compare_or_fusion) | copy-start | bytes 1732
  88.1 6.0 %collective-permute-start.1 = (bf16[288,3,128]{2,0,1:T(8,128)(2,1)S(1)}, bf16[288,3,128]{2,0,1:T(8,128)(2,1)S(1)}, u32[]{:S(2)}, u32[]{:S(2)}) collective-permute-start(bf16[288,3,128]{2,0,1:T(8,128)(2,1)S(1)} %copy.37), channel_id=1, source_target_pairs={{0,8},{4,12},{8,0},{12,4},{16,24},{20,28},{24,16},{28,20},{1,9},{5... | collective-permute-start | bytes 663560 | tf_op jit(solution)/shard_map/ppermute | solution.py:23
  89.2 7.2 %collective-permute-start = (bf16[288,3,128]{2,0,1:T(8,128)(2,1)S(1)}, bf16[288,3,128]{2,0,1:T(8,128)(2,1)S(1)}, u32[]{:S(2)}, u32[]{:S(2)}) collective-permute-start(bf16[288,3,128]{2,0,1:T(8,128)(2,1)S(1)} %fusion.52), channel_id=1, source_target_pairs={{0,8},{4,12},{8,0},{12,4},{16,24},{20,28},{24,16},{28,20},{1,9},{5... | collective-permute-start | bytes 663560 | tf_op jit(solution)/shard_map/ppermute | solution.py:23
  97.1 217.9 %copy-start.10 = (f32[3072]{0:T(1024)S(1)}, f32[3072]{0:T(1024)}, u32[]{:S(2)}) copy-start(f32[3072]{0:T(1024)} %copy-done.9) | copy-start | bytes 36868
  97.1 217.9 %copy-start.12 = (f32[3072]{0:T(1024)S(1)}, f32[3072]{0:T(1024)}, u32[]{:S(2)}) copy-start(f32[3072]{0:T(1024)} %copy-done.11) | copy-start | bytes 36868
  97.2 217.9 %copy-start.14 = (f32[288]{0:T(512)S(1)}, f32[288]{0:T(512)}, u32[]{:S(2)}) copy-start(f32[288]{0:T(512)} %copy-done.13) | copy-start | bytes 3460
  97.2 217.9 %copy-start.19 = (f32[288]{0:T(512)S(1)}, f32[288]{0:T(512)}, u32[]{:S(2)}) copy-start(f32[288]{0:T(512)} %copy-done.18) | copy-start | bytes 3460
  329.6 6.5 %copy-start.24 = (bf16[288,3,128]{2,0,1:T(8,128)(2,1)S(1)}, bf16[288,3,128]{2,0,1:T(8,128)(2,1)}, u32[]{:S(2)}) copy-start(bf16[288,3,128]{2,0,1:T(8,128)(2,1)} %copy-done.23) | copy-start | bytes 663556
  333.9 42.9 %copy-start.2 = (bf16[288,768]{1,0:T(8,128)(2,1)S(1)}, bf16[288,768]{1,0:T(8,128)(2,1)}, u32[]{:S(2)}) copy-start(bf16[288,768]{1,0:T(8,128)(2,1)} %param.16) | copy-start | bytes 1327108
  337.5 101.6 %copy-start.7 = (f32[144,64]{0,1:T(8,128)S(1)}, f32[144,64]{0,1:T(8,128)}, u32[]{:S(2)}) copy-start(f32[144,64]{0,1:T(8,128)} %param.17) | copy-start | bytes 110596
  378.8 61.7 %copy-start.4 = (bf16[288,768]{1,0:T(8,128)(2,1)}, bf16[288,768]{1,0:T(8,128)(2,1)S(1)}, u32[]{:S(2)}) copy-start(bf16[288,768]{1,0:T(8,128)(2,1)S(1)} %get-tuple-element.71) | copy-start | bytes 1327108
  435.1 4.0 collective-permute-start.2
  (10 other events, 31.3 us)
Sparse Core Ops, SparseCore 0:
  9.6 23.7 all-gather.5
  35.5 140.9 all-gather.9
  178.7 136.2 all-gather.7
  334.1 27.6 reduce-scatter.1
where the time goes:
time: 448 us; the launch traced here: 447 us
  waiting for transfers between devices  223 us (50%)
  blocking collectives  133 us (30%)
  matrix products  32.8 us (7%)
  other arithmetic  20.7 us (5%)
  local copies, waits for them, and re-layouts  19.9 us (4%)
  between operations  14.9 us (3%)
    all_gather x1, waiting for transfers between devices, body(): lax.all_gather(w_mlp_in, 'seq', axis=0, tiled=True)  138 us
    all_gather x1, waiting for transfers between devices, body(): lax.all_gather(w_mlp_down, 'seq', axis=0, tiled=True)  77.2 us
    all_gather x2, blocking collectives, merged(): pieces = jax.tree.map(lambda part: lax.all_gather(part, axis), value)  74.8 us
    all_gather x1, blocking collectives, body(): modulation = lax.all_gather(summed_mod, 'seq', axis=1, tiled=True)  31.3 us
    dot_general x1, matrix products, down_product(): lax.dot_general(hidden_rows, weight_rows, (((1,), (1,)), ((), ())), prefe...  14.6 us
    unnamed x55, local copies, waits for them, and re-layouts  11.3 us
    psum x1, blocking collectives, body(): lax.psum(velocity_part.astype(jnp.bfloat16), 'tp').astype(jnp.float32)  10.6 us
    psum x1, blocking collectives, body(): summed_mod = lax.psum(partial_mod, 'tp')  9.05 us
  transfers between devices with their start and end apart: 7, of which 5 were waited for; matrix products, arithmetic and copies ran while one was open for 11% of the time, Pallas kernels for 0%

commit v1 on v0

--- a/solution.py
+++ b/solution.py
@@ -23,12 +23,66 @@
     return lax.ppermute(value, axis, [(i, i ^ 1 << apart) for i in range(lax.axis_size(axis))])
 
 
-def merged(value, axis, join):
-    pieces = jax.tree.map(lambda part: lax.all_gather(part, axis), value)
-    head = jax.tree.map(lambda part: part[0], pieces)
-    tail = jax.tree.map(lambda part: part[1:], pieces)
-    total, _ = lax.scan(lambda total, section: (join(total, section), None), head, tail)
-    return total
+def crossed(value, axis, mask):
+    pairs = [(i, i ^ mask) for i in range(lax.axis_size(axis))]
+    return jax.tree.map(lambda part: lax.ppermute(part, axis, pairs), value)
+
+
+def summed(value, axis):
+    mask = 1
+    while mask < lax.axis_size(axis):
+        value = jax.tree.map(jnp.add, value, crossed(value, axis, mask))
+        mask *= 2
+    return value
+
+
+def placed(pieces, index, count):
+    shape = pieces[0].shape
+    buffer = jnp.zeros((count,) + shape, pieces[0].dtype)
+    for mask, piece in pieces.items():
+        buffer = lax.dynamic_update_slice(
+            buffer, piece[None], (index ^ mask,) + (0,) * len(shape)
+        )
+    return buffer
+
+
+def spread(pieces, axis, mask):
+    while mask:
+        for held in list(pieces):
+            pieces[held | mask] = crossed(pieces[held], axis, mask)
+        mask //= 2
+    return pieces
+
+
+def gathered_small(value, axis):
+    count = lax.axis_size(axis)
+    return placed(spread({0: value}, axis, count // 2), lax.axis_index(axis), count)
+
+
+def gathered_half(weight, axis):
+    count = lax.axis_size(axis)
+    index = lax.axis_index(axis)
+    top = count // 2
+    side = index // top
+    width = weight.shape[1] // 2
+    keep = lax.dynamic_slice_in_dim(weight, side * width, width, 1)
+    give = lax.dynamic_slice_in_dim(weight, (1 - side) * width, width, 1)
+    pieces = spread({0: keep, top: crossed(give, axis, top)}, axis, top // 2)
+    return placed(pieces, index, count).reshape(count * weight.shape[0], width)
+
+
+def scattered(term, axis):
+    index = lax.axis_index(axis)
+    core, side = index % 2, index // 2
+    quarters = jnp.split(term, 4, axis=1)
+    keep = [jnp.where(core == 0, quarters[i], quarters[i + 1]) for i in (0, 2)]
+    give = [
+        jnp.where(core == 0, quarters[i + 1], quarters[i]).astype(jnp.bfloat16) for i in (0, 2)
+    ]
+    got = crossed(give, axis, 1)
+    low, high = [mine + other.astype(jnp.float32) for mine, other in zip(keep, got)]
+    give = jnp.where(side == 0, high, low).astype(jnp.bfloat16)
+    return jnp.where(side == 0, low, high) + crossed(give, axis, 2).astype(jnp.float32)
 
 
 def sigma_of(step_count):
@@ -72,10 +126,6 @@
     second = paired[..., 1]
     turned = jnp.stack([first * cosine - second * sine, first * sine + second * cosine], axis=-1)
     return turned.reshape(count, heads_here, size)
-
-
-def combine_stats(first_pair, second_pair):
-    return (first_pair[0] + second_pair[0], jnp.maximum(first_pair[1], second_pair[1]))
 
 
 def down_product(hidden_rows, weight_rows):
@@ -114,28 +164,36 @@
     time_vec = jax.nn.silu(time_embedding(sigma_now)).astype(jnp.bfloat16)
     time_rows = lax.dynamic_slice_in_dim(time_vec, tp_index * width_tp, width_tp, 1)
     partial_mod = jnp.dot(time_rows, w_mod, preferred_element_type=jnp.float32)
-    summed_mod = lax.psum(partial_mod, "tp")
-    modulation = lax.all_gather(summed_mod, "seq", axis=1, tiled=True)
+    final_total = jnp.sum(w_final.astype(jnp.float32), axis=0)
+    summed_mod, final_total = summed((partial_mod, final_total), "tp")
+    modulation = gathered_small(summed_mod, "seq").transpose(1, 0, 2).reshape(REQ, 3 * D)
     own_mod = jnp.sum(jnp.where(request_pick[:, None], modulation, 0.0), axis=0)
-    shift_vec = own_mod[:D]
-    scale_vec = own_mod[D : 2 * D]
+    far_mod = jnp.sum(jnp.where(request_pick[:, None], 0.0, modulation), axis=0)
     gate_vec = lax.dynamic_slice_in_dim(own_mod[2 * D :], tp_index * width_tp, width_tp, 0)
-    full_rows = lax.all_gather(state, "tp", axis=1, tiled=True)
-    modded = ((1.0 + scale_vec) * layer_norm(full_rows.astype(jnp.float32)) + shift_vec).astype(
-        jnp.bfloat16
-    )
+    far_bit = lax.axis_size("seq") // 2
+    far_state = crossed(state, "seq", far_bit)
+
+    def modulated(part, vec):
+        rows = lax.all_gather(part, "tp", axis=1, tiled=True).astype(jnp.float32)
+        return ((1.0 + vec[D : 2 * D]) * layer_norm(rows) + vec[:D]).astype(jnp.bfloat16)
+
+    modded = modulated(state, own_mod)
+    far_modded = modulated(far_state, far_mod)
     heads_here = w_qkv.shape[2] // HD
     projected = jnp.dot(
         modded, w_qkv.reshape(D, 3 * heads_here * HD), preferred_element_type=jnp.float32
     )
     projected = projected.reshape(TOK_DEV, 3, heads_here, HD)
     mlp_pre = jnp.dot(
-        modded,
-        lax.all_gather(w_mlp_in, "seq", axis=0, tiled=True),
+        jnp.concatenate([far_modded, modded], axis=0),
+        gathered_half(w_mlp_in, "seq"),
         preferred_element_type=jnp.float32,
     )
     mlp_hidden = jax.nn.gelu(mlp_pre, approximate=True).astype(jnp.bfloat16)
-    mlp_term = down_product(mlp_hidden, lax.all_gather(w_mlp_down, "seq", axis=0, tiled=True))
+    down_rows = gathered_half(w_mlp_down, "seq")
+    far_term = down_product(mlp_hidden[:TOK_DEV], down_rows)
+    mlp_term = down_product(mlp_hidden[TOK_DEV:], down_rows)
+    far_update = crossed(scattered(far_term, "tp").astype(jnp.bfloat16), "seq", far_bit)
     angles = rope_angles(rope_ids)
     queries = rotate(rms_norm(projected[:, 0]) * q_gain[None], angles).astype(jnp.bfloat16)
     key_rows = rotate(rms_norm(projected[:, 1]) * k_gain[None], angles).astype(jnp.bfloat16)
@@ -166,19 +224,21 @@
     attended = jnp.einsum("hqk,khd->qhd", weights, value_rows, preferred_element_type=jnp.float32)
     attended = attended.astype(jnp.bfloat16).reshape(TOK_DEV, heads_here * HD)
     term = jnp.dot(attended, w_out, preferred_element_type=jnp.float32) + mlp_term
-    update = lax.psum_scatter(
-        term.astype(jnp.bfloat16), "tp", scatter_dimension=1, tiled=True
-    ).astype(jnp.float32)
+    update = scattered(term, "tp") + far_update.astype(jnp.float32)
     new_state = (state.astype(jnp.float32) + gate_vec * update).astype(jnp.bfloat16)
     state_values = new_state.astype(jnp.float32)
-    row_total, row_squares = lax.psum(
-        (jnp.sum(state_values, axis=1), jnp.sum(state_values * state_values, axis=1)), "tp"
-    )
-    row_mean = (row_total / D)[:, None]
-    row_var = (row_squares / D)[:, None] - row_mean * row_mean
-    normed_out = ((state_values - row_mean) * lax.rsqrt(row_var + NORM_EPS)).astype(jnp.bfloat16)
-    velocity_part = jnp.dot(normed_out, w_final, preferred_element_type=jnp.float32)
-    velocity = lax.psum(velocity_part.astype(jnp.bfloat16), "tp").astype(jnp.float32)
+    row_total = jnp.sum(state_values, axis=1, keepdims=True)
+    row_squares = jnp.sum(state_values * state_values, axis=1, keepdims=True)
+    raw_velocity = jnp.dot(new_state, w_final, preferred_element_type=jnp.float32)
+    tail = jnp.concatenate(
+        [raw_velocity, row_total, row_squares, jnp.zeros((TOK_DEV, 62), jnp.float32)], axis=1
+    )
+    tail = summed(tail, "tp")
+    channels = w_final.shape[1]
+    row_mean = tail[:, channels : channels + 1] / D
+    row_squares = tail[:, channels + 1 : channels + 2]
+    row_var = row_squares / D - row_mean * row_mean
+    velocity = (tail[:, :channels] - row_mean * final_total) * lax.rsqrt(row_var + NORM_EPS)
     half_rows = TOK_DEV // 2
     keep_part = lax.dynamic_slice_in_dim(velocity, guided_half * half_rows, half_rows, 0)
     give_part = lax.dynamic_slice_in_dim(velocity, (1 - guided_half) * half_rows, half_rows, 0)
@@ -188,9 +248,13 @@
     guide_scale = jnp.sum(jnp.where(request_pick, guidance, 0)).astype(jnp.float32) / 2.0
     own_step = jnp.sum(jnp.where(request_pick, step_size, 0.0))
     next_latent = latent + own_step * (uncond_part + guide_scale * (cond_part - uncond_part))
-    square_vec = jnp.where(request_pick, jnp.sum(state_values * state_values), 0.0)
-    peak_vec = jnp.where(request_pick, top_local, MASKED_SCORE)
-    square_total, top_score = merged((square_vec, peak_vec), ("seq", "tp"), combine_stats)
+    square_total = summed(jnp.where(request_pick, jnp.sum(row_squares), 0.0), "seq")
+    top_score = jnp.where(request_pick, top_local, MASKED_SCORE)
+    for axis in ("tp", "seq"):
+        mask = 1
+        while mask < lax.axis_size(axis):
+            top_score = jnp.maximum(top_score, crossed(top_score, axis, mask))
+            mask *= 2
     state_norm = jnp.sqrt(square_total / (2.0 * seq_len * D))
     return (new_state, next_latent, state_norm, top_score)
 

time: 448 us -> 322 us (0.72)
  blocking collectives: 133 us -> 0 us
  waiting for transfers between devices: 223 us -> 152 us
  starting transfers between devices: 2.37 us -> 36.6 us
  local copies, waits for them, and re-layouts: 19.9 us -> 47.6 us
  other arithmetic: 20.7 us -> 37.8 us
    all_gather x3 -> x2, waiting for transfers between devices: 216 us -> 0.01 us  [modulated(): rows = lax.all_gather(part, 'tp', axis=1, tiled=True).astype(jnp.float32)]
    ppermute x0 -> x43, waiting for transfers between devices: none -> 149 us  [crossed(): return jax.tree.map(lambda part: lax.ppermute(part, axis, pairs), value)]
    all_gather x3 -> x0, blocking collectives: 106 us -> none  [the longest x2 74.8 us: merged(): pieces = jax.tree.map(lambda part: lax.all_gather(part, axis), value)]
    ppermute x0 -> x43, starting transfers between devices: none -> 33.8 us  [crossed(): return jax.tree.map(lambda part: lax.ppermute(part, axis, pairs), value)]
    psum x3 -> x0, blocking collectives: 26.9 us -> none  [the longest x1 10.6 us: body(): lax.psum(velocity_part.astype(jnp.bfloat16), 'tp').astype(jnp.float32)]
    dynamic_update_slice x0 -> x23, local copies, waits for them, and re-layouts: none -> 19.7 us  [placed(): lax.dynamic_update_slice(buffer, piece[None], (index ^ mask,) + (0,) * le...]
    dot_general x1 -> x2, matrix products: 14.6 us -> 8 us  [down_product(): lax.dot_general(hidden_rows, weight_rows, (((1,), (1,)), ((), ())), prefe...]
    another operation x0 -> x2, local copies, waits for them, and re-layouts: none -> 5.18 us
  transfers between devices with their start and end apart: 7 -> 48, of which waited for: 5 -> 29; matrix products, arithmetic and copies ran while one was open for 11% -> 30% of each run, Pallas kernels for 0% -> 0%
where the time goes in v1:
time: 322 us; the launch traced here: 320 us
  waiting for transfers between devices  152 us (47%)
  local copies, waits for them, and re-layouts  47.6 us (15%)
  other arithmetic  37.8 us (12%)
  starting transfers between devices  36.6 us (11%)
  matrix products  30.8 us (10%)
  between operations  15.4 us (5%)
    ppermute x43, waiting for transfers between devices, crossed(): return jax.tree.map(lambda part: lax.ppermute(part, axis, pairs), value)  149 us
    ppermute x43, starting transfers between devices, crossed(): return jax.tree.map(lambda part: lax.ppermute(part, axis, pairs), value)  33.8 us
    dynamic_update_slice x23, local copies, waits for them, and re-layouts, placed(): lax.dynamic_update_slice(buffer, piece[None], (index ^ mask,) + (0,) * le...  19.7 us
    unnamed x55, local copies, waits for them, and re-layouts  10.4 us
    dot_general x2, matrix products, down_product(): lax.dot_general(hidden_rows, weight_rows, (((1,), (1,)), ((), ())), prefe...  8 us
  transfers between devices with their start and end apart: 48, of which 29 were waited for; matrix products, arithmetic and copies ran while one was open for 30% of the time, Pallas kernels for 0%

profile of v1, /device:TPU:0, one launch (start us, length us, event | category | flops | bytes accessed | tf_op | source)
XLA Modules:
  0.0 320.3 jit_solution(15739937119697065626)
XLA Ops:
  37.3 10.3 %copy.18 = bf16[3072,3,384]{0,2,1:T(8,128)(2,1)} copy(bf16[3072,3,384]{2,0,1:T(8,128)(2,1)} %param.17) | data formatting | bytes 14155776 | tf_op args[3]
  49.1 13.9 %collective-permute-done.2 = f32[2,1152]{1,0:T(2,128)S(1)} collective-permute-done((f32[2,1152]{1,0:T(2,128)S(1)}, f32[2,1152]{1,0:T(2,128)S(1)}, u32[]{:S(2)}, u32[]{:S(2)}) %collective-permute-start.2) | collective-permute-done | bytes 9248 | tf_op jit(solution)/shard_map/ppermute | solution.py:28
  63.0 3.7 %collective-permute-done.3 = f32[2,1152]{1,0:T(2,128)S(1)} collective-permute-done((f32[2,1152]{1,0:T(2,128)S(1)}, f32[2,1152]{1,0:T(2,128)S(1)}, u32[]{:S(2)}, u32[]{:S(2)}) %collective-permute-start.3) | collective-permute-done | bytes 9248 | tf_op jit(solution)/shard_map/ppermute | solution.py:28
  66.7 3.7 %collective-permute-done.4 = f32[2,1152]{1,0:T(2,128)S(1)} collective-permute-done((f32[2,1152]{1,0:T(2,128)S(1)}, f32[2,1152]{1,0:T(2,128)S(1)}, u32[]{:S(2)}, u32[]{:S(2)}) %collective-permute-start.4) | collective-permute-done | bytes 9248 | tf_op jit(solution)/shard_map/ppermute | solution.py:28
  81.9 3.2 %collective-permute-done.8 = f32[2,1152]{1,0:T(2,128)S(1)} collective-permute-done((f32[2,1152]{1,0:T(2,128)S(1)}, f32[2,1152]{1,0:T(2,128)S(1)}, u32[]{:S(2)}, u32[]{:S(2)}) %collective-permute-start.8) | collective-permute-done | bytes 9248 | tf_op jit(solution)/shard_map/ppermute | solution.py:28
  94.3 11.7 %collective-permute-done.12 = bf16[384,768]{1,0:T(8,128)(2,1)} collective-permute-done((bf16[384,768]{1,0:T(8,128)(2,1)}, bf16[384,768]{1,0:T(8,128)(2,1)}, u32[]{:S(2)}, u32[]{:S(2)}) %collective-permute-start.12) | collective-permute-done | bytes 589856 | tf_op jit(solution)/shard_map/ppermute | solution.py:28
  108.4 4.9 %collective-permute-done.13 = bf16[384,768]{1,0:T(8,128)(2,1)} collective-permute-done((bf16[384,768]{1,0:T(8,128)(2,1)}, bf16[384,768]{1,0:T(8,128)(2,1)}, u32[]{:S(2)}, u32[]{:S(2)}) %collective-permute-start.13) | collective-permute-done | bytes 589856 | tf_op jit(solution)/shard_map/ppermute | solution.py:28
  115.8 7.0 %collective-permute-done.21 = bf16[384,768]{1,0:T(8,128)(2,1)S(1)} collective-permute-done((bf16[384,768]{1,0:T(8,128)(2,1)}, bf16[384,768]{1,0:T(8,128)(2,1)S(1)}, u32[]{:S(2)}, u32[]{:S(2)}) %collective-permute-start.21) | collective-permute-done | bytes 589856 | tf_op jit(solution)/shard_map/ppermute | solution.py:28
  128.5 4.4 %collective-permute-done.14 = bf16[384,768]{1,0:T(8,128)(2,1)S(1)} collective-permute-done((bf16[384,768]{1,0:T(8,128)(2,1)}, bf16[384,768]{1,0:T(8,128)(2,1)S(1)}, u32[]{:S(2)}, u32[]{:S(2)}) %collective-permute-start.14) | collective-permute-done | bytes 589856 | tf_op jit(solution)/shard_map/ppermute | solution.py:28
  137.6 10.1 %collective-permute-done.16 = bf16[384,768]{1,0:T(8,128)(2,1)S(1)} collective-permute-done((bf16[384,768]{1,0:T(8,128)(2,1)}, bf16[384,768]{1,0:T(8,128)(2,1)S(1)}, u32[]{:S(2)}, u32[]{:S(2)}) %collective-permute-start.16) | collective-permute-done | bytes 589856 | tf_op jit(solution)/shard_map/ppermute | solution.py:28
  148.6 11.8 %collective-permute-done.17 = bf16[384,768]{1,0:T(8,128)(2,1)S(1)} collective-permute-done((bf16[384,768]{1,0:T(8,128)(2,1)}, bf16[384,768]{1,0:T(8,128)(2,1)S(1)}, u32[]{:S(2)}, u32[]{:S(2)}) %collective-permute-start.17) | collective-permute-done | bytes 589856 | tf_op jit(solution)/shard_map/ppermute | solution.py:28
  161.2 11.8 %collective-permute-done.25 = bf16[384,768]{1,0:T(8,128)(2,1)S(1)} collective-permute-done((bf16[384,768]{1,0:T(8,128)(2,1)S(1)}, bf16[384,768]{1,0:T(8,128)(2,1)S(1)}, u32[]{:S(2)}, u32[]{:S(2)}) %collective-permute-start.25) | collective-permute-done | bytes 589856 | tf_op jit(solution)/shard_map/ppermute | solution.py:28
  173.8 7.9 %collective-permute-done.18 = bf16[384,768]{1,0:T(8,128)(2,1)S(1)} collective-permute-done((bf16[384,768]{1,0:T(8,128)(2,1)S(1)}, bf16[384,768]{1,0:T(8,128)(2,1)S(1)}, u32[]{:S(2)}, u32[]{:S(2)}) %collective-permute-start.18) | collective-permute-done | bytes 589856 | tf_op jit(solution)/shard_map/ppermute | solution.py:28
  187.5 5.4 %fusion.25 = f32[288,3,3,128]{3,0,2,1:T(8,128)S(1)} fusion(bf16[3,3,128,3072]{3,2,1,0:T(8,128)(2,1)} %bitcast.90, bf16[288,3072]{1,0:T(8,128)(2,1)S(1)} %fusion.12), kind=kOutput, calls=%fused_computation.34 | convolution fusion | flops 2038431744 | bytes 10174464 | tf_op jit(solution)/shard_map/dot_general | solution.py:183
  225.1 5.5 %fusion.24 = bf16[576,768]{1,0:T(8,128)(2,1)S(1)} fusion(bf16[3072,768]{1,0:T(8,128)(2,1)} %bitcast.23, bf16[288,3072]{1,0:T(8,128)(2,1)S(1)} %copy-done.11, bf16[288,3072]{1,0:T(8,128)(2,1)S(1)} %fusion.8), kind=kOutput, calls=%fused_computation.33 | convolution fusion | flops 2728968192 | bytes 9142272 | tf_op jit(solution)/shard_map/dot_general | solution.py:187
  230.6 4.1 %fusion.36 = f32[288,3072]{1,0:T(8,128)S(1)} fusion(bf16[3072,768]{1,0:T(8,128)(2,1)} %bitcast.32, bf16[576,768]{1,0:T(8,128)(2,1)S(1)} %fusion.24), kind=kOutput, calls=%fused_computation.76 | convolution fusion | flops 1358954496 | bytes 8699904 | tf_op jit(solution)/shard_map/dot_general | solution.py:132
  235.4 3.9 %convolution_add_fusion = f32[288,3072]{1,0:T(8,128)S(1)} fusion(f32[288,3072]{1,0:T(8,128)S(1)} %copy-done.3, bf16[3072,768]{1,0:T(8,128)(2,1)} %bitcast.32, bf16[576,768]{1,0:T(8,128)(2,1)S(1)} %fusion.24), kind=kOutput, calls=%fused_computation.9 | convolution fusion | flops 1359839232 | bytes 12238848 | tf_op jit(solution)/shard_map/dot_general | solution.py:132
  244.7 9.1 %collective-permute-done.31 = bf16[288,768]{1,0:T(8,128)(2,1)S(1)} collective-permute-done((bf16[288,768]{1,0:T(8,128)(2,1)S(1)}, bf16[288,768]{1,0:T(8,128)(2,1)S(1)}, u32[]{:S(2)}, u32[]{:S(2)}) %collective-permute-start.31) | collective-permute-done | bytes 442400 | tf_op jit(solution)/shard_map/ppermute | solution.py:28
  259.1 3.4 %collective-permute-done.36 = f32[64]{0:T(128)S(1)} collective-permute-done((f32[64]{0:T(128)S(1)}, f32[64]{0:T(128)S(1)}, u32[]{:S(2)}, u32[]{:S(2)}) %collective-permute-start.36) | collective-permute-done | bytes 288 | tf_op jit(solution)/shard_map/ppermute | solution.py:28
  266.6 9.4 %collective-permute-done.32 = bf16[288,768]{1,0:T(8,128)(2,1)} collective-permute-done((bf16[288,768]{1,0:T(8,128)(2,1)}, bf16[288,768]{1,0:T(8,128)(2,1)}, u32[]{:S(2)}, u32[]{:S(2)}) %collective-permute-start.32) | collective-permute-done | bytes 442400 | tf_op jit(solution)/shard_map/ppermute | solution.py:28
  288.0 3.5 %collective-permute-done.44 = f32[2]{0:T(128)S(1)} collective-permute-done((f32[2]{0:T(128)S(1)}, f32[2]{0:T(128)S(1)}, u32[]{:S(2)}, u32[]{:S(2)}) %collective-permute-start.44) | collective-permute-done | bytes 40 | tf_op jit(solution)/shard_map/ppermute | solution.py:28
  291.8 4.2 %collective-permute-done.45 = f32[2]{0:T(128)S(1)} collective-permute-done((f32[2]{0:T(128)S(1)}, f32[2]{0:T(128)S(1)}, u32[]{:S(2)}, u32[]{:S(2)}) %collective-permute-start.45) | collective-permute-done | bytes 40 | tf_op jit(solution)/shard_map/ppermute | solution.py:28
  302.9 3.5 %collective-permute-done.39 = f32[2]{0:T(128)S(1)} collective-permute-done((f32[2]{0:T(128)S(1)}, f32[2]{0:T(128)S(1)}, u32[]{:S(2)}, u32[]{:S(2)}) %collective-permute-start.39) | collective-permute-done | bytes 40 | tf_op jit(solution)/shard_map/ppermute | solution.py:28
  307.4 4.2 %collective-permute-done.40 = f32[2]{0:T(128)S(1)} collective-permute-done((f32[2]{0:T(128)S(1)}, f32[2]{0:T(128)S(1)}, u32[]{:S(2)}, u32[]{:S(2)}) %collective-permute-start.40) | collective-permute-done | bytes 40 | tf_op jit(solution)/shard_map/ppermute | solution.py:28
  (247 shorter events, 144.4 us)
Async XLA Ops:
  7.2 175.4 %all-gather.3.cloned.1.call-start = ((), (), s32[]{:S(2)}) async-start(), calls=%async_computation | async-start | bytes 2211840 | tf_op jit(solution)/shard_map/all_gather | solution.py:177
  10.9 81.4 %collective-permute-start.20 = (bf16[384,768]{1,0:T(8,128)(2,1)S(1)}, bf16[384,768]{1,0:T(8,128)(2,1)}, u32[]{:S(2)}, u32[]{:S(2)}) collective-permute-start(bf16[384,768]{1,0:T(8,128)(2,1)S(1)} %get-tuple-element.24), channel_id=1, source_target_pairs={{0,8},{4,12},{8,0},{12,4},{16,24},{20,28},{24,16},{28,20},{1,9},{5... | collective-permute-start | bytes 1769480 | tf_op jit(solution)/shard_map/ppermute | solution.py:28
  13.9 109.8 %collective-permute-start.22 = (bf16[384,768]{1,0:T(8,128)(2,1)S(1)}, bf16[384,768]{1,0:T(8,128)(2,1)}, u32[]{:S(2)}, u32[]{:S(2)}) collective-permute-start(bf16[384,768]{1,0:T(8,128)(2,1)S(1)} %get-tuple-element.24), channel_id=1, source_target_pairs={{0,4},{4,0},{8,12},{12,8},{16,20},{20,16},{24,28},{28,24},{1,5},{5... | collective-permute-start | bytes 1769480 | tf_op jit(solution)/shard_map/ppermute | solution.py:28
  15.4 204.8 %all-gather.5.cloned.1.call-start = ((), (), s32[]{:S(2)}) async-start(), calls=%async_computation.1 | async-start | bytes 2211840 | tf_op jit(solution)/shard_map/all_gather | solution.py:177
  15.5 72.2 %collective-permute-start.11 = (bf16[288,768]{1,0:T(8,128)(2,1)S(1)}, bf16[288,768]{1,0:T(8,128)(2,1)}, u32[]{:S(2)}, u32[]{:S(2)}) collective-permute-start(bf16[288,768]{1,0:T(8,128)(2,1)S(1)} %copy-done.6), channel_id=1, source_target_pairs={{0,16},{4,20},{8,24},{12,28},{16,0},{20,4},{24,8},{28,12},{1,17},{... | collective-permute-start | bytes 1327112 | tf_op jit(solution)/shard_map/ppermute | solution.py:28
  20.1 69.7 %collective-permute-start.19 = (bf16[384,768]{1,0:T(8,128)(2,1)}, bf16[384,768]{1,0:T(8,128)(2,1)}, u32[]{:S(2)}, u32[]{:S(2)}) collective-permute-start(bf16[384,768]{1,0:T(8,128)(2,1)} %constant_dynamic-slice_fusion), channel_id=1, source_target_pairs={{0,16},{4,20},{8,24},{12,28},{16,0},{20,4},{24,8},{28,12},{1,17},{... | collective-permute-start | bytes 1769480 | tf_op jit(solution)/shard_map/ppermute | solution.py:28
  34.6 28.4 %collective-permute-start.2 = (f32[2,1152]{1,0:T(2,128)S(1)}, f32[2,1152]{1,0:T(2,128)S(1)}, u32[]{:S(2)}, u32[]{:S(2)}) collective-permute-start(f32[2,1152]{1,0:T(2,128)S(1)} %get-tuple-element.20), channel_id=1, source_target_pairs={{0,16},{4,20},{8,24},{12,28},{16,0},{20,4},{24,8},{28,12},{1,17},{... | collective-permute-start | bytes 27656 | tf_op jit(solution)/shard_map/ppermute | solution.py:28
  85.2 20.8 %collective-permute-start.12 = (bf16[384,768]{1,0:T(8,128)(2,1)}, bf16[384,768]{1,0:T(8,128)(2,1)}, u32[]{:S(2)}, u32[]{:S(2)}) collective-permute-start(bf16[384,768]{1,0:T(8,128)(2,1)} %constant_dynamic-slice_fusion.2), channel_id=1, source_target_pairs={{0,16},{4,20},{8,24},{12,28},{16,0},{20,4},{24,8},{28,12},{1,17},{... | collective-permute-start | bytes 1769480 | tf_op jit(solution)/shard_map/ppermute | solution.py:28
  87.7 25.5 %collective-permute-start.13 = (bf16[384,768]{1,0:T(8,128)(2,1)}, bf16[384,768]{1,0:T(8,128)(2,1)}, u32[]{:S(2)}, u32[]{:S(2)}) collective-permute-start(bf16[384,768]{1,0:T(8,128)(2,1)} %get-tuple-element.22), channel_id=1, source_target_pairs={{0,8},{4,12},{8,0},{12,4},{16,24},{20,28},{24,16},{28,20},{1,9},{5... | collective-permute-start | bytes 1769480 | tf_op jit(solution)/shard_map/ppermute | solution.py:28
  89.8 46.9 %collective-permute-start.15 = (bf16[384,768]{1,0:T(8,128)(2,1)}, bf16[384,768]{1,0:T(8,128)(2,1)S(1)}, u32[]{:S(2)}, u32[]{:S(2)}) collective-permute-start(bf16[384,768]{1,0:T(8,128)(2,1)} %get-tuple-element.22), channel_id=1, source_target_pairs={{0,4},{4,0},{8,12},{12,8},{16,20},{20,16},{24,28},{28,24},{1,5},{5... | collective-permute-start | bytes 1769480 | tf_op jit(solution)/shard_map/ppermute | solution.py:28
  92.3 30.5 %collective-permute-start.21 = (bf16[384,768]{1,0:T(8,128)(2,1)}, bf16[384,768]{1,0:T(8,128)(2,1)S(1)}, u32[]{:S(2)}, u32[]{:S(2)}) collective-permute-start(bf16[384,768]{1,0:T(8,128)(2,1)} %collective-permute-done.19), channel_id=1, source_target_pairs={{0,8},{4,12},{8,0},{12,4},{16,24},{20,28},{24,16},{28,20},{1,9},{5... | collective-permute-start | bytes 1769480 | tf_op jit(solution)/shard_map/ppermute | solution.py:28
  105.9 20.3 %collective-permute-start.23 = (bf16[384,768]{1,0:T(8,128)(2,1)}, bf16[384,768]{1,0:T(8,128)(2,1)S(1)}, u32[]{:S(2)}, u32[]{:S(2)}) collective-permute-start(bf16[384,768]{1,0:T(8,128)(2,1)} %collective-permute-done.19), channel_id=1, source_target_pairs={{0,4},{4,0},{8,12},{12,8},{16,20},{20,16},{24,28},{28,24},{1,5},{5... | collective-permute-start | bytes 1769480 | tf_op jit(solution)/shard_map/ppermute | solution.py:28
  113.3 21.8 %collective-permute-start.24 = (bf16[384,768]{1,0:T(8,128)(2,1)}, bf16[384,768]{1,0:T(8,128)(2,1)S(1)}, u32[]{:S(2)}, u32[]{:S(2)}) collective-permute-start(bf16[384,768]{1,0:T(8,128)(2,1)} %collective-permute-done.20), channel_id=1, source_target_pairs={{0,4},{4,0},{8,12},{12,8},{16,20},{20,16},{24,28},{28,24},{1,5},{5... | collective-permute-start | bytes 1769480 | tf_op jit(solution)/shard_map/ppermute | solution.py:28
  122.8 10.1 %collective-permute-start.14 = (bf16[384,768]{1,0:T(8,128)(2,1)}, bf16[384,768]{1,0:T(8,128)(2,1)S(1)}, u32[]{:S(2)}, u32[]{:S(2)}) collective-permute-start(bf16[384,768]{1,0:T(8,128)(2,1)} %collective-permute-done.12), channel_id=1, source_target_pairs={{0,8},{4,12},{8,0},{12,4},{16,24},{20,28},{24,16},{28,20},{1,9},{5... | collective-permute-start | bytes 1769480 | tf_op jit(solution)/shard_map/ppermute | solution.py:28
  123.7 24.0 %collective-permute-start.16 = (bf16[384,768]{1,0:T(8,128)(2,1)}, bf16[384,768]{1,0:T(8,128)(2,1)S(1)}, u32[]{:S(2)}, u32[]{:S(2)}) collective-permute-start(bf16[384,768]{1,0:T(8,128)(2,1)} %collective-permute-done.12), channel_id=1, source_target_pairs={{0,4},{4,0},{8,12},{12,8},{16,20},{20,16},{24,28},{28,24},{1,5},{5... | collective-permute-start | bytes 1769480 | tf_op jit(solution)/shard_map/ppermute | solution.py:28
  126.2 34.1 %collective-permute-start.17 = (bf16[384,768]{1,0:T(8,128)(2,1)}, bf16[384,768]{1,0:T(8,128)(2,1)S(1)}, u32[]{:S(2)}, u32[]{:S(2)}) collective-permute-start(bf16[384,768]{1,0:T(8,128)(2,1)} %collective-permute-done.13), channel_id=1, source_target_pairs={{0,4},{4,0},{8,12},{12,8},{16,20},{20,16},{24,28},{28,24},{1,5},{5... | collective-permute-start | bytes 1769480 | tf_op jit(solution)/shard_map/ppermute | solution.py:28
  132.9 40.1 %collective-permute-start.25 = (bf16[384,768]{1,0:T(8,128)(2,1)S(1)}, bf16[384,768]{1,0:T(8,128)(2,1)S(1)}, u32[]{:S(2)}, u32[]{:S(2)}) collective-permute-start(bf16[384,768]{1,0:T(8,128)(2,1)S(1)} %collective-permute-done.21), channel_id=1, source_target_pairs={{0,4},{4,0},{8,12},{12,8},{16,20},{20,16},{24,28},{28,24},{1,5},{5... | collective-permute-start | bytes 1769480 | tf_op jit(solution)/shard_map/ppermute | solution.py:28
  135.1 46.7 %collective-permute-start.18 = (bf16[384,768]{1,0:T(8,128)(2,1)S(1)}, bf16[384,768]{1,0:T(8,128)(2,1)S(1)}, u32[]{:S(2)}, u32[]{:S(2)}) collective-permute-start(bf16[384,768]{1,0:T(8,128)(2,1)S(1)} %collective-permute-done.14), channel_id=1, source_target_pairs={{0,4},{4,0},{8,12},{12,8},{16,20},{20,16},{24,28},{28,24},{1,5},{5... | collective-permute-start | bytes 1769480 | tf_op jit(solution)/shard_map/ppermute | solution.py:28
  240.7 13.1 %collective-permute-start.31 = (bf16[288,768]{1,0:T(8,128)(2,1)S(1)}, bf16[288,768]{1,0:T(8,128)(2,1)S(1)}, u32[]{:S(2)}, u32[]{:S(2)}) collective-permute-start(bf16[288,768]{1,0:T(8,128)(2,1)S(1)} %select_convert_fusion), channel_id=1, source_target_pairs={{0,2},{1,3},{2,0},{3,1},{4,6},{5,7},{6,4},{7,5},{8,10},{9,11},{10,... | collective-permute-start | bytes 1327112 | tf_op jit(solution)/shard_map/ppermute | solution.py:28
  243.4 23.2 %collective-permute-start.28 = (bf16[288,768]{1,0:T(8,128)(2,1)}, bf16[288,768]{1,0:T(8,128)(2,1)}, u32[]{:S(2)}, u32[]{:S(2)}) collective-permute-start(bf16[288,768]{1,0:T(8,128)(2,1)} %select_convert_fusion.3), channel_id=1, source_target_pairs={{0,2},{1,3},{2,0},{3,1},{4,6},{5,7},{6,4},{7,5},{8,10},{9,11},{10,... | collective-permute-start | bytes 1327112 | tf_op jit(solution)/shard_map/ppermute | solution.py:28
  254.9 21.1 %collective-permute-start.32 = (bf16[288,768]{1,0:T(8,128)(2,1)}, bf16[288,768]{1,0:T(8,128)(2,1)}, u32[]{:S(2)}, u32[]{:S(2)}) collective-permute-start(bf16[288,768]{1,0:T(8,128)(2,1)} %add_convert_fusion.1), channel_id=1, source_target_pairs={{0,16},{4,20},{8,24},{12,28},{16,0},{20,4},{24,8},{28,12},{1,17},{... | collective-permute-start | bytes 1327112 | tf_op jit(solution)/shard_map/ppermute | solution.py:28
  266.6 12.9 %collective-permute-start.41 = (f32[2]{0:T(128)S(1)}, f32[2]{0:T(128)S(1)}, u32[]{:S(2)}, u32[]{:S(2)}) collective-permute-start(f32[2]{0:T(128)S(1)} %broadcast_select_fusion), channel_id=1, source_target_pairs={{0,1},{1,0},{2,3},{3,2},{4,5},{5,4},{6,7},{7,6},{8,9},{9,8},{10,11... | collective-permute-start | bytes 32 | tf_op jit(solution)/shard_map/ppermute | solution.py:28
  281.8 14.7 %collective-permute-start.34 = (f32[288,128]{0,1:T(8,128)S(1)}, f32[288,128]{0,1:T(8,128)S(1)}, u32[]{:S(2)}, u32[]{:S(2)}) collective-permute-start(f32[288,128]{0,1:T(8,128)S(1)} %fusion.78), channel_id=1, source_target_pairs={{0,2},{1,3},{2,0},{3,1},{4,6},{5,7},{6,4},{7,5},{8,10},{9,11},{10,... | collective-permute-start | bytes 442376 | tf_op jit(solution)/shard_map/ppermute | solution.py:28
  297.3 14.8 %collective-permute-start.37 = (bf16[144,64]{0,1:T(8,128)(2,1)S(1)}, bf16[144,64]{0,1:T(8,128)(2,1)S(1)}, u32[]{:S(2)}, u32[]{:S(2)}) collective-permute-start(bf16[144,64]{0,1:T(8,128)(2,1)S(1)} %dynamic-slice_convert_fusion), channel_id=1, source_target_pairs={{0,4},{4,0},{8,12},{12,8},{16,20},{20,16},{24,28},{28,24},{1,5},{5... | collective-permute-start | bytes 55304 | tf_op jit(solution)/shard_map/ppermute | solution.py:23
  (51 other events, 623.2 us)
Sparse Core Ops, SparseCore 0:
  15.6 20.1 all-gather.2
  89.9 18.7 all-gather.4

commit v2 on v1

--- a/solution.py
+++ b/solution.py
@@ -1,8 +1,11 @@
+import functools
 import math
 
 import jax
 import jax.numpy as jnp
 from jax import lax
+from jax.experimental import pallas as pl
+from jax.experimental.pallas import tpu as pltpu
 from jax.sharding import PartitionSpec as P
 
 D = 3072
@@ -36,39 +39,182 @@
     return value
 
 
-def placed(pieces, index, count):
-    shape = pieces[0].shape
-    buffer = jnp.zeros((count,) + shape, pieces[0].dtype)
-    for mask, piece in pieces.items():
-        buffer = lax.dynamic_update_slice(
-            buffer, piece[None], (index ^ mask,) + (0,) * len(shape)
-        )
-    return buffer
-
-
-def spread(pieces, axis, mask):
-    while mask:
-        for held in list(pieces):
-            pieces[held | mask] = crossed(pieces[held], axis, mask)
-        mask //= 2
-    return pieces
-
-
-def gathered_small(value, axis):
-    count = lax.axis_size(axis)
-    return placed(spread({0: value}, axis, count // 2), lax.axis_index(axis), count)
-
-
-def gathered_half(weight, axis):
-    count = lax.axis_size(axis)
-    index = lax.axis_index(axis)
-    top = count // 2
-    side = index // top
-    width = weight.shape[1] // 2
-    keep = lax.dynamic_slice_in_dim(weight, side * width, width, 1)
-    give = lax.dynamic_slice_in_dim(weight, (1 - side) * width, width, 1)
-    pieces = spread({0: keep, top: crossed(give, axis, top)}, axis, top // 2)
-    return placed(pieces, index, count).reshape(count * weight.shape[0], width)
+def head_kernel(
+    n, w_in, w_down, state, mod, in_all, down_half, rows, far, mod_all, mod_parts,
+    own_sem, w_send, w_recv, s_send, s_recv, m_send, m_recv,
+):
+    seq, tp = lax.axis_index("seq"), lax.axis_index("tp")
+    top = n // 2
+    side = seq // top
+    width = w_in.shape[1] // 2
+    depth = state.shape[1]
+    bits = [1 << k for k in reversed(range(n.bit_length() - 1))]
+
+    def column(index, size):
+        return pl.ds(pl.multiple_of(index * size, size), size)
+
+    def remote(src, dst, send, recv, to_seq, to_tp):
+        return pltpu.make_async_remote_copy(
+            src_ref=src, dst_ref=dst, send_sem=send, recv_sem=recv,
+            device_id=(to_seq, to_tp), device_id_type=pl.DeviceIdType.MESH,
+        )
+
+    barrier = pltpu.get_barrier_semaphore()
+    for bit in bits:
+        pl.semaphore_signal(
+            barrier, device_id=(seq ^ bit, tp), device_id_type=pl.DeviceIdType.MESH
+        )
+    for other in (1, 2, 3):
+        pl.semaphore_signal(
+            barrier, device_id=(seq, tp ^ other), device_id_type=pl.DeviceIdType.MESH
+        )
+    pl.semaphore_wait(barrier, len(bits) + 3)
+
+    started = []
+
+    def go(copy):
+        copy.start()
+        started.append(copy)
+        return copy
+
+    def slot(which, mask):
+        return in_all.at[seq ^ mask] if which == 0 else down_half.at[(seq ^ mask) // 2]
+
+    def send_piece(which, mask, bit, src):
+        return go(
+            remote(
+                src, slot(which, mask), w_send.at[which, mask, bit.bit_length() - 1],
+                w_recv.at[which, mask | bit], seq ^ bit, tp,
+            )
+        )
+
+    def lowest(which):
+        return (1, 2)[which]
+
+    def forward(which, mask, src, below):
+        for bit in bits:
+            if lowest(which) <= bit < below:
+                send_piece(which, mask, bit, src)
+
+    for other in (1, 2, 3):
+        go(remote(mod, mod_parts.at[other], m_send.at[other], m_recv.at[other], seq, tp ^ other))
+    go(remote(state, far.at[:, column(tp, depth)], s_send.at[4], s_recv.at[4], seq ^ top, tp))
+    for other in (1, 2, 3):
+        go(
+            remote(
+                state, rows.at[:, column(tp, depth)], s_send.at[other], s_recv.at[other],
+                seq, tp ^ other,
+            )
+        )
+    weights = (w_in, w_down)
+    for which in (0, 1):
+        far_half = weights[which].at[:, column(1 - side, width)]
+        near_half = weights[which].at[:, column(side, width)]
+        go_far = remote(
+            far_half, slot(which, 0), w_send.at[which, 0, top.bit_length() - 1],
+            w_recv.at[which, top], seq ^ top, tp,
+        )
+        go(go_far)
+        forward(which, 0, near_half, top)
+    local = [
+        pltpu.make_async_copy(
+            weights[which].at[:, column(side, width)], slot(which, 0), own_sem.at[which]
+        )
+        for which in (0, 1)
+    ]
+    local.append(
+        pltpu.make_async_copy(state, rows.at[:, column(tp, depth)], own_sem.at[2])
+    )
+    for copy in local:
+        copy.start()
+
+    total = mod[...]
+    for other in (1, 2, 3):
+        part = mod_parts.at[other]
+        remote(mod, part, m_send.at[other], m_recv.at[other], seq, tp ^ other).wait_recv()
+        total = total + mod_parts[other]
+    mod_all[seq] = total
+    for level in range(n.bit_length() - 1):
+        size = 1 << level
+        mine = mod_all.at[pl.ds(seq // size * size, size)]
+        theirs = mod_all.at[pl.ds((seq ^ size) // size * size, size)]
+        go(remote(mine, mine, m_send.at[4 + level], m_recv.at[4 + level], seq ^ size, tp))
+        remote(
+            mine, theirs, m_send.at[4 + level], m_recv.at[4 + level], seq ^ size, tp
+        ).wait_recv()
+
+    def arrive(which, mask):
+        place = slot(which, mask)
+        bit = mask & -mask
+        remote(
+            place, place, w_send.at[which, mask, 0], w_recv.at[which, mask], seq ^ bit, tp
+        ).wait_recv()
+
+    done_far = False
+    for bit in bits:
+        masks = [mask for mask in range(n) if mask & -mask == bit]
+        for mask in masks:
+            for which in (0, 1):
+                if bit >= lowest(which):
+                    arrive(which, mask)
+                    forward(which, mask, slot(which, mask), bit)
+            if not done_far:
+                done_far = True
+                piece = far.at[:, column(tp, depth)]
+                remote(piece, piece, s_send.at[4], s_recv.at[4], seq ^ top, tp).wait_recv()
+                for other in (1, 2, 3):
+                    go(
+                        remote(
+                            piece, piece, s_send.at[4 + other], s_recv.at[4 + other],
+                            seq, tp ^ other,
+                        )
+                    )
+    for other in (1, 2, 3):
+        for base, target in ((0, rows), (4, far)):
+            piece = target.at[:, column(tp ^ other, depth)]
+            remote(
+                piece, piece, s_send.at[base + other], s_recv.at[base + other], seq, tp ^ other
+            ).wait_recv()
+    for copy in started:
+        copy.wait_send()
+    for copy in local:
+        copy.wait()
+
+
+def head_exchange(w_in, w_down, state, mod):
+    n = lax.axis_size("seq")
+    levels = n.bit_length() - 1
+    deep, wide = w_in.shape
+    tokens, depth = state.shape
+    kind = jax.ShapeDtypeStruct
+    anywhere = pl.BlockSpec(memory_space=pl.ANY)
+    vmem = pl.BlockSpec(memory_space=pltpu.VMEM)
+    dma = pltpu.SemaphoreType.DMA
+    return pl.pallas_call(
+        functools.partial(head_kernel, n),
+        out_shape=(
+            kind((n, deep, wide // 2), w_in.dtype),
+            kind((n // 2, deep, wide // 2), w_down.dtype),
+            kind((tokens, 4 * depth), state.dtype),
+            kind((tokens, 4 * depth), state.dtype),
+            kind((n,) + mod.shape, mod.dtype),
+        ),
+        in_specs=[anywhere, anywhere, anywhere, vmem],
+        out_specs=(anywhere, anywhere, anywhere, anywhere, vmem),
+        scratch_shapes=[
+            pltpu.VMEM((4,) + mod.shape, mod.dtype),
+            dma((3,)),
+            dma((2, n, levels)),
+            dma((2, n)),
+            dma((8,)),
+            dma((8,)),
+            dma((4 + levels,)),
+            dma((4 + levels,)),
+        ],
+        compiler_params=pltpu.CompilerParams(
+            collective_id=0, has_side_effects=True, vmem_limit_bytes=16 * 1024 * 1024
+        ),
+    )(w_in, w_down, state, mod)
 
 
 def scattered(term, axis):
@@ -165,20 +311,29 @@
     time_rows = lax.dynamic_slice_in_dim(time_vec, tp_index * width_tp, width_tp, 1)
     partial_mod = jnp.dot(time_rows, w_mod, preferred_element_type=jnp.float32)
     final_total = jnp.sum(w_final.astype(jnp.float32), axis=0)
-    summed_mod, final_total = summed((partial_mod, final_total), "tp")
-    modulation = gathered_small(summed_mod, "seq").transpose(1, 0, 2).reshape(REQ, 3 * D)
+    mod_width = partial_mod.shape[1]
+    channels = w_final.shape[1]
+    extra = jnp.zeros((REQ, -(mod_width + channels) % 128), jnp.float32)
+    packed = jnp.concatenate(
+        [partial_mod, jnp.broadcast_to(final_total, (REQ, channels)), extra], axis=1
+    )
+    in_all, down_half, full_rows, far_rows, mod_all = head_exchange(
+        w_mlp_in, w_mlp_down, state, packed
+    )
+    other_half = crossed(down_half, "seq", 1)
+    modulation = mod_all[:, :, :mod_width].transpose(1, 0, 2).reshape(REQ, 3 * D)
+    final_total = mod_all[0, 0, mod_width : mod_width + channels]
     own_mod = jnp.sum(jnp.where(request_pick[:, None], modulation, 0.0), axis=0)
     far_mod = jnp.sum(jnp.where(request_pick[:, None], 0.0, modulation), axis=0)
     gate_vec = lax.dynamic_slice_in_dim(own_mod[2 * D :], tp_index * width_tp, width_tp, 0)
     far_bit = lax.axis_size("seq") // 2
-    far_state = crossed(state, "seq", far_bit)
 
     def modulated(part, vec):
-        rows = lax.all_gather(part, "tp", axis=1, tiled=True).astype(jnp.float32)
+        rows = part.astype(jnp.float32)
         return ((1.0 + vec[D : 2 * D]) * layer_norm(rows) + vec[:D]).astype(jnp.bfloat16)
 
-    modded = modulated(state, own_mod)
-    far_modded = modulated(far_state, far_mod)
+    modded = modulated(full_rows, own_mod)
+    far_modded = modulated(far_rows, far_mod)
     heads_here = w_qkv.shape[2] // HD
     projected = jnp.dot(
         modded, w_qkv.reshape(D, 3 * heads_here * HD), preferred_element_type=jnp.float32
@@ -186,11 +341,13 @@
     projected = projected.reshape(TOK_DEV, 3, heads_here, HD)
     mlp_pre = jnp.dot(
         jnp.concatenate([far_modded, modded], axis=0),
-        gathered_half(w_mlp_in, "seq"),
+        in_all.reshape(D, in_all.shape[2]),
         preferred_element_type=jnp.float32,
     )
     mlp_hidden = jax.nn.gelu(mlp_pre, approximate=True).astype(jnp.bfloat16)
-    down_rows = gathered_half(w_mlp_down, "seq")
+    even = jnp.where(guided_half == 0, down_half, other_half)
+    odd = jnp.where(guided_half == 0, other_half, down_half)
+    down_rows = jnp.stack([even, odd], axis=1).reshape(D, down_half.shape[2])
     far_term = down_product(mlp_hidden[:TOK_DEV], down_rows)
     mlp_term = down_product(mlp_hidden[TOK_DEV:], down_rows)
     far_update = crossed(scattered(far_term, "tp").astype(jnp.bfloat16), "seq", far_bit)
@@ -230,11 +387,12 @@
     row_total = jnp.sum(state_values, axis=1, keepdims=True)
     row_squares = jnp.sum(state_values * state_values, axis=1, keepdims=True)
     raw_velocity = jnp.dot(new_state, w_final, preferred_element_type=jnp.float32)
+    peaks = jnp.where(jnp.arange(62) == tp_index, top_local, 0.0)
     tail = jnp.concatenate(
-        [raw_velocity, row_total, row_squares, jnp.zeros((TOK_DEV, 62), jnp.float32)], axis=1
+        [raw_velocity, row_total, row_squares, jnp.broadcast_to(peaks, (TOK_DEV, 62))], axis=1
     )
     tail = summed(tail, "tp")
-    channels = w_final.shape[1]
+    top_local = jnp.max(tail[0, channels + 2 : channels + 6])
     row_mean = tail[:, channels : channels + 1] / D
     row_squares = tail[:, channels + 1 : channels + 2]
     row_var = row_squares / D - row_mean * row_mean
@@ -248,13 +406,14 @@
     guide_scale = jnp.sum(jnp.where(request_pick, guidance, 0)).astype(jnp.float32) / 2.0
     own_step = jnp.sum(jnp.where(request_pick, step_size, 0.0))
     next_latent = latent + own_step * (uncond_part + guide_scale * (cond_part - uncond_part))
-    square_total = summed(jnp.where(request_pick, jnp.sum(row_squares), 0.0), "seq")
+    square_total = jnp.where(request_pick, jnp.sum(row_squares), 0.0)
     top_score = jnp.where(request_pick, top_local, MASKED_SCORE)
-    for axis in ("tp", "seq"):
-        mask = 1
-        while mask < lax.axis_size(axis):
-            top_score = jnp.maximum(top_score, crossed(top_score, axis, mask))
-            mask *= 2
+    mask = 1
+    while mask < lax.axis_size("seq"):
+        other = crossed(jnp.concatenate([square_total, top_score]), "seq", mask)
+        square_total = square_total + other[:REQ]
+        top_score = jnp.maximum(top_score, other[REQ:])
+        mask *= 2
     state_norm = jnp.sqrt(square_total / (2.0 * seq_len * D))
     return (new_state, next_latent, state_norm, top_score)
 

time: 322 us -> 272 us (0.84)
  Pallas kernels: 0 us -> 119 us
  waiting for transfers between devices: 152 us -> 43.7 us
  starting transfers between devices: 36.6 us -> 9.24 us
  local copies, waits for them, and re-layouts: 47.6 us -> 30.9 us
  between operations: 15.4 us -> 1.84 us
  matrix products: 30.8 us -> 26.8 us
    pallas_call x0 -> x1, Pallas kernels: none -> 119 us  [head_exchange(): pl.pallas_call(functools.partial(head_kernel, n), out_shape=(kind((n, dee...]
    ppermute x43 -> x13, waiting for transfers between devices: 149 us -> 43.7 us  [crossed(): return jax.tree.map(lambda part: lax.ppermute(part, axis, pairs), value)]
    ppermute x43 -> x13, starting transfers between devices: 33.8 us -> 5.59 us  [crossed(): return jax.tree.map(lambda part: lax.ppermute(part, axis, pairs), value)]
    dynamic_update_slice x23 -> x0, local copies, waits for them, and re-layouts: 19.7 us -> none  [placed(): lax.dynamic_update_slice(buffer, piece[None], (index ^ mask,) + (0,) * le...]
    unnamed x55 -> x43, local copies, waits for them, and re-layouts: 10.4 us -> 18.2 us
    another operation x2 -> x1, local copies, waits for them, and re-layouts: 5.18 us -> 0.31 us  [body(): down_rows = jnp.stack([even, odd], axis=1).reshape(D, down_half.shape[2])]
    dot_general x2, matrix products: 8 us -> 3.14 us  [down_product(): lax.dot_general(hidden_rows, weight_rows, (((1,), (1,)), ((), ())), prefe...]
    dynamic_slice x2 -> x0, local copies, waits for them, and re-layouts: 3.98 us -> none  [gathered_half(): give = lax.dynamic_slice_in_dim(weight, (1 - side) * width, width, 1)]
  transfers between devices with their start and end apart: 48 -> 16, of which waited for: 29 -> 10; matrix products, arithmetic and copies ran while one was open for 30% -> 27% of each run, Pallas kernels for 0% -> 0%
where the time goes in v2:
time: 272 us; the launch traced here: 270 us
  Pallas kernels  119 us (44%)
  waiting for transfers between devices  43.7 us (16%)
  other arithmetic  39.1 us (14%)
  local copies, waits for them, and re-layouts  30.9 us (11%)
  matrix products  26.8 us (10%)
  starting transfers between devices  9.24 us (3%)
    pallas_call x1, Pallas kernels, head_exchange(): pl.pallas_call(functools.partial(head_kernel, n), out_shape=(kind((n, dee...  119 us
    ppermute x13, waiting for transfers between devices, crossed(): return jax.tree.map(lambda part: lax.ppermute(part, axis, pairs), value)  43.7 us
    unnamed x43, local copies, waits for them, and re-layouts  18.2 us
    dot_general x1, matrix products, body(): jnp.dot(jnp.concatenate([far_modded, modded], axis=0), in_all.reshape(D,...  6.38 us
    ppermute x13, starting transfers between devices, crossed(): return jax.tree.map(lambda part: lax.ppermute(part, axis, pairs), value)  5.59 us
  transfers between devices with their start and end apart: 16, of which 10 were waited for; matrix products, arithmetic and copies ran while one was open for 27% of the time, Pallas kernels for 0%

profile of v2, /device:TPU:0, one launch (start us, length us, event | category | flops | bytes accessed | tf_op | source)
XLA Modules:
  0.0 270.4 jit_solution(2339842224765744515)
XLA Ops:
  3.5 2.4 fusion.64
  9.6 118.8 %shard_map.165 = (bf16[8,384,768]{2,1,0:T(8,128)(2,1)S(1)}, bf16[4,384,768]{2,1,0:T(8,128)(2,1)}, bf16[288,3072]{1,0:T(8,128)(2,1)S(1)}, bf16[288,3072]{1,0:T(8,128)(2,1)S(1)}, f32[8,2,1280]{2,1,0:T(2,128)S(1)}) custom-call(bf16[384,1536]{1,0:T(8,128)(2,1)S(1)} %copy-done.7, bf16[384,1536]{1,0:T(8,128)(2,1)S(1)} %copy-done.8, ...), custom_call_target="tpu_custom_call" | custom-call | tf_op jit(solution)/shard_map/pallas_call | solution.py:193
  130.9 2.2 copy-done.10
  136.1 1.8 convert_reduce_fusion.1
  138.5 10.3 %copy.18 = bf16[3072,3,384]{0,2,1:T(8,128)(2,1)} copy(bf16[3072,3,384]{2,0,1:T(8,128)(2,1)} %param.17) | data formatting | bytes 14155776 | tf_op args[3]
  148.8 2.3 fusion.12
  151.1 5.4 %fusion.25 = f32[288,3,3,128]{3,0,2,1:T(8,128)S(1)} fusion(bf16[3,3,128,3072]{3,2,1,0:T(8,128)(2,1)} %bitcast.49, bf16[288,3072]{1,0:T(8,128)(2,1)S(1)} %fusion.12), kind=kOutput, calls=%fused_computation.37 | convolution fusion | flops 2038431744 | bytes 10174464 | tf_op jit(solution)/shard_map/dot_general | solution.py:338
  156.5 1.8 multiply_reduce_fusion
  161.8 2.1 copy.19
  175.7 2.1 collective-permute-start
  178.5 1.9 convert_reduce_fusion
  182.8 2.3 fusion.8
  185.1 6.4 %fusion.24 = bf16[576,768]{1,0:T(8,128)(2,1)} fusion(bf16[3072,768]{1,0:T(8,128)(2,1)} %bitcast.48, bf16[288,3072]{1,0:T(8,128)(2,1)S(1)} %copy-done.13, bf16[288,3072]{1,0:T(8,128)(2,1)S(1)} %fusion.8), kind=kOutput, calls=%fused_computation.36 | convolution fusion | flops 2728968192 | bytes 9142272 | tf_op jit(solution)/shard_map/dot_general | solution.py:342
  192.2 3.4 %fusion.81 = (f32[3,288]{1,0:T(4,128)S(1)}, f32[3,288,576]{2,1,0:T(8,128)}) fusion(pred[576]{0:T(1024)(128)(4,1)S(1)} %compare_or_fusion, bf16[288,3,128]{0,2,1:T(8,128)(2,1)S(1)} %convert_element_type.151, bf16[288,3,128]{2,0,1:T(8,128)(2,1)} %collective-permute-done.1, bf16[288,3,128]{2,0,1:T(8,128)(2,1)} %copy.22), kind=kOutput, calls=%fused_computation.169 | convolution fusion | flops 130277952 | bytes 2658240 | tf_op jit(solution)/shard_map/sub | solution.py:379
  195.6 2.1 fusion.31
  197.8 2.7 select_bitcast_fusion.1
  210.9 10.6 %collective-permute-done.8 = bf16[288,768]{1,0:T(8,128)(2,1)S(1)} collective-permute-done((bf16[288,768]{1,0:T(8,128)(2,1)S(1)}, bf16[288,768]{1,0:T(8,128)(2,1)S(1)}, u32[]{:S(2)}, u32[]{:S(2)}) %collective-permute-start.8) | collective-permute-done | bytes 442400 | tf_op jit(solution)/shard_map/ppermute | solution.py:31
  223.4 2.4 fusion.27
  226.6 3.6 %collective-permute-done.5 = bf16[288,768]{1,0:T(8,128)(2,1)S(1)} collective-permute-done((bf16[288,768]{1,0:T(8,128)(2,1)S(1)}, bf16[288,768]{1,0:T(8,128)(2,1)S(1)}, u32[]{:S(2)}, u32[]{:S(2)}) %collective-permute-start.5) | collective-permute-done | bytes 442400 | tf_op jit(solution)/shard_map/ppermute | solution.py:31
  230.1 12.3 %collective-permute-done.9 = bf16[288,768]{1,0:T(8,128)(2,1)S(1)} collective-permute-done((bf16[288,768]{1,0:T(8,128)(2,1)S(1)}, bf16[288,768]{1,0:T(8,128)(2,1)S(1)}, u32[]{:S(2)}, u32[]{:S(2)}) %collective-permute-start.9) | collective-permute-done | bytes 442400 | tf_op jit(solution)/shard_map/ppermute | solution.py:31
  246.7 5.6 %collective-permute-done.11 = f32[288,128]{0,1:T(8,128)S(1)} collective-permute-done((f32[288,128]{0,1:T(8,128)S(1)}, f32[288,128]{0,1:T(8,128)S(1)}, u32[]{:S(2)}, u32[]{:S(2)}) %collective-permute-start.11) | collective-permute-done | bytes 147488 | tf_op jit(solution)/shard_map/ppermute | solution.py:31
  257.2 3.0 %collective-permute-done.13 = f32[4]{0:T(128)S(1)} collective-permute-done((f32[4]{0:T(128)S(1)}, f32[4]{0:T(128)S(1)}, u32[]{:S(2)}, u32[]{:S(2)}) %collective-permute-start.13) | collective-permute-done | bytes 48 | tf_op jit(solution)/shard_map/ppermute | solution.py:31
  260.3 3.5 %collective-permute-done.14 = f32[4]{0:T(128)S(1)} collective-permute-done((f32[4]{0:T(128)S(1)}, f32[4]{0:T(128)S(1)}, u32[]{:S(2)}, u32[]{:S(2)}) %collective-permute-start.14) | collective-permute-done | bytes 48 | tf_op jit(solution)/shard_map/ppermute | solution.py:31
  264.5 3.9 %collective-permute-done.15 = f32[4]{0:T(128)S(1)} collective-permute-done((f32[4]{0:T(128)S(1)}, f32[4]{0:T(128)S(1)}, u32[]{:S(2)}, u32[]{:S(2)}) %collective-permute-start.15) | collective-permute-done | bytes 48 | tf_op jit(solution)/shard_map/ppermute | solution.py:31
  (145 shorter events, 55.8 us)
Async XLA Ops:
  0.6 205.3 %copy-start = (bf16[384,3072]{1,0:T(8,128)(2,1)S(1)}, bf16[384,3072]{1,0:T(8,128)(2,1)}, u32[]{:S(2)}) copy-start(bf16[384,3072]{1,0:T(8,128)(2,1)} %param.21) | copy-start | bytes 7077892
  0.6 6.6 %copy-start.7 = (bf16[384,1536]{1,0:T(8,128)(2,1)S(1)}, bf16[384,1536]{1,0:T(8,128)(2,1)}, u32[]{:S(2)}) copy-start(bf16[384,1536]{1,0:T(8,128)(2,1)} %w_in.1) | copy-start | bytes 3538948
  133.1 64.7 %collective-permute-start.2 = (bf16[4,384,768]{2,1,0:T(8,128)(2,1)}, bf16[4,384,768]{2,1,0:T(8,128)(2,1)}, u32[]{:S(2)}, u32[]{:S(2)}) collective-permute-start(bf16[4,384,768]{2,1,0:T(8,128)(2,1)} %get-tuple-element.13), channel_id=1, source_target_pairs={{0,4},{4,0},{8,12},{12,8},{16,20},{20,16},{24,28},{28,24},{1,5},{5... | collective-permute-start | bytes 7077896 | tf_op jit(solution)/shard_map/ppermute | solution.py:31
  151.1 5.4 %copy-start.12 = (bf16[288,3072]{1,0:T(8,128)(2,1)}, bf16[288,3072]{1,0:T(8,128)(2,1)S(1)}, u32[]{:S(2)}) copy-start(bf16[288,3072]{1,0:T(8,128)(2,1)S(1)} %fusion.12) | copy-start | bytes 5308420
  174.6 17.6 %collective-permute-start.1 = (bf16[288,3,128]{2,0,1:T(8,128)(2,1)}, bf16[288,3,128]{2,0,1:T(8,128)(2,1)}, u32[]{:S(2)}, u32[]{:S(2)}) collective-permute-start(bf16[288,3,128]{2,0,1:T(8,128)(2,1)} %copy.22), channel_id=1, source_target_pairs={{0,8},{4,12},{8,0},{12,4},{16,24},{20,28},{24,16},{28,20},{1,9},{5... | collective-permute-start | bytes 663560 | tf_op jit(solution)/shard_map/ppermute | solution.py:26
  175.7 19.9 %collective-permute-start = (bf16[288,3,128]{2,0,1:T(8,128)(2,1)S(1)}, bf16[288,3,128]{2,0,1:T(8,128)(2,1)}, u32[]{:S(2)}, u32[]{:S(2)}) collective-permute-start(bf16[288,3,128]{2,0,1:T(8,128)(2,1)S(1)} %fusion.51), channel_id=1, source_target_pairs={{0,8},{4,12},{8,0},{12,4},{16,24},{20,28},{24,16},{28,20},{1,9},{5... | collective-permute-start | bytes 663560 | tf_op jit(solution)/shard_map/ppermute | solution.py:26
  205.4 2.7 collective-permute-start.6
  205.5 2.6 collective-permute-start.7
  207.5 1.9 collective-permute-start.3
  207.6 2.3 collective-permute-start.4
  208.4 13.1 %collective-permute-start.8 = (bf16[288,768]{1,0:T(8,128)(2,1)S(1)}, bf16[288,768]{1,0:T(8,128)(2,1)S(1)}, u32[]{:S(2)}, u32[]{:S(2)}) collective-permute-start(bf16[288,768]{1,0:T(8,128)(2,1)S(1)} %select_convert_fusion), channel_id=1, source_target_pairs={{0,2},{1,3},{2,0},{3,1},{4,6},{5,7},{6,4},{7,5},{8,10},{9,11},{10,... | collective-permute-start | bytes 1327112 | tf_op jit(solution)/shard_map/ppermute | solution.py:31
  210.3 19.8 %collective-permute-start.5 = (bf16[288,768]{1,0:T(8,128)(2,1)S(1)}, bf16[288,768]{1,0:T(8,128)(2,1)S(1)}, u32[]{:S(2)}, u32[]{:S(2)}) collective-permute-start(bf16[288,768]{1,0:T(8,128)(2,1)S(1)} %select_convert_fusion.3), channel_id=1, source_target_pairs={{0,2},{1,3},{2,0},{3,1},{4,6},{5,7},{6,4},{7,5},{8,10},{9,11},{10,... | collective-permute-start | bytes 1327112 | tf_op jit(solution)/shard_map/ppermute | solution.py:31
  222.0 20.4 %copy-start.6 = (bf16[288,768]{1,0:T(8,128)(2,1)S(1)}, bf16[288,768]{1,0:T(8,128)(2,1)}, u32[]{:S(2)}) copy-start(bf16[288,768]{1,0:T(8,128)(2,1)} %state.1) | copy-start | bytes 1327108
  222.0 20.4 %collective-permute-start.9 = (bf16[288,768]{1,0:T(8,128)(2,1)S(1)}, bf16[288,768]{1,0:T(8,128)(2,1)S(1)}, u32[]{:S(2)}, u32[]{:S(2)}) collective-permute-start(bf16[288,768]{1,0:T(8,128)(2,1)S(1)} %add_convert_fusion.1), channel_id=1, source_target_pairs={{0,16},{4,20},{8,24},{12,28},{16,0},{20,4},{24,8},{28,12},{1,17},{... | collective-permute-start | bytes 1327112 | tf_op jit(solution)/shard_map/ppermute | solution.py:31
  226.6 16.5 %copy-start.15 = (bf16[768,64]{0,1:T(8,128)(2,1)S(1)}, bf16[768,64]{0,1:T(8,128)(2,1)}, u32[]{:S(2)}) copy-start(bf16[768,64]{0,1:T(8,128)(2,1)} %param.23) | copy-start | bytes 294916
  226.6 17.0 %copy-start.19 = (s32[2]{0:T(128)S(1)}, s32[2]{0:T(128)}, u32[]{:S(2)}) copy-start(s32[2]{0:T(128)} %param.26) | copy-start | bytes 28
  243.0 27.4 %copy-start.11 = (bf16[288,768]{1,0:T(8,128)(2,1)}, bf16[288,768]{1,0:T(8,128)(2,1)S(1)}, u32[]{:S(2)}) copy-start(bf16[288,768]{1,0:T(8,128)(2,1)S(1)} %get-tuple-element.28) | copy-start | bytes 1327108
  243.0 26.0 %copy-start.16 = (f32[144,64]{0,1:T(8,128)S(1)}, f32[144,64]{0,1:T(8,128)}, u32[]{:S(2)}) copy-start(f32[144,64]{0,1:T(8,128)} %param.15) | copy-start | bytes 110596
  243.4 1.5 collective-permute-start.10
  245.0 7.3 %collective-permute-start.11 = (f32[288,128]{0,1:T(8,128)S(1)}, f32[288,128]{0,1:T(8,128)S(1)}, u32[]{:S(2)}, u32[]{:S(2)}) collective-permute-start(f32[288,128]{0,1:T(8,128)S(1)} %fusion.79), channel_id=1, source_target_pairs={{0,2},{1,3},{2,0},{3,1},{4,6},{5,7},{6,4},{7,5},{8,10},{9,11},{10,... | collective-permute-start | bytes 442376 | tf_op jit(solution)/shard_map/ppermute | solution.py:31
  253.7 15.4 %collective-permute-start.12 = (bf16[144,64]{0,1:T(8,128)(2,1)S(1)}, bf16[144,64]{0,1:T(8,128)(2,1)S(1)}, u32[]{:S(2)}, u32[]{:S(2)}) collective-permute-start(bf16[144,64]{0,1:T(8,128)(2,1)S(1)} %dynamic-slice_convert_fusion), channel_id=1, source_target_pairs={{0,4},{4,0},{8,12},{12,8},{16,20},{20,16},{24,28},{28,24},{1,5},{5... | collective-permute-start | bytes 55304 | tf_op jit(solution)/shard_map/ppermute | solution.py:26
  256.6 3.5 %collective-permute-start.13 = (f32[4]{0:T(128)S(1)}, f32[4]{0:T(128)S(1)}, u32[]{:S(2)}, u32[]{:S(2)}) collective-permute-start(f32[4]{0:T(128)S(1)} %pad_maximum_fusion.4), channel_id=1, source_target_pairs={{0,4},{4,0},{8,12},{12,8},{16,20},{20,16},{24,28},{28,24},{1,5},{5... | collective-permute-start | bytes 56 | tf_op jit(solution)/shard_map/ppermute | solution.py:31
  260.3 3.5 %collective-permute-start.14 = (f32[4]{0:T(128)S(1)}, f32[4]{0:T(128)S(1)}, u32[]{:S(2)}, u32[]{:S(2)}) collective-permute-start(f32[4]{0:T(128)S(1)} %pad_maximum_fusion.5), channel_id=1, source_target_pairs={{0,8},{4,12},{8,0},{12,4},{16,24},{20,28},{24,16},{28,20},{1,9},{5... | collective-permute-start | bytes 56 | tf_op jit(solution)/shard_map/ppermute | solution.py:31
  264.0 4.4 %collective-permute-start.15 = (f32[4]{0:T(128)S(1)}, f32[4]{0:T(128)S(1)}, u32[]{:S(2)}, u32[]{:S(2)}) collective-permute-start(f32[4]{0:T(128)S(1)} %pad_maximum_fusion.6), channel_id=1, source_target_pairs={{0,16},{4,20},{8,24},{12,28},{16,0},{20,4},{24,8},{28,12},{1,17},{... | collective-permute-start | bytes 56 | tf_op jit(solution)/shard_map/ppermute | solution.py:31
  (13 other events, 24.9 us)

commit v3 on v2

--- a/solution.py
+++ b/solution.py
@@ -78,7 +78,7 @@
         return copy
 
     def slot(which, mask):
-        return in_all.at[seq ^ mask] if which == 0 else down_half.at[(seq ^ mask) // 2]
+        return in_all.at[seq ^ mask] if which == 0 else down_half.at[(seq ^ mask) // top]
 
     def send_piece(which, mask, bit, src):
         return go(
@@ -89,7 +89,7 @@
         )
 
     def lowest(which):
-        return (1, 2)[which]
+        return (1, top)[which]
 
     def forward(which, mask, src, below):
         for bit in bits:
@@ -194,7 +194,7 @@
         functools.partial(head_kernel, n),
         out_shape=(
             kind((n, deep, wide // 2), w_in.dtype),
-            kind((n // 2, deep, wide // 2), w_down.dtype),
+            kind((2, deep, wide // 2), w_down.dtype),
             kind((tokens, 4 * depth), state.dtype),
             kind((tokens, 4 * depth), state.dtype),
             kind((n,) + mod.shape, mod.dtype),
@@ -215,6 +215,14 @@
             collective_id=0, has_side_effects=True, vmem_limit_bytes=16 * 1024 * 1024
         ),
     )(w_in, w_down, state, mod)
+
+
+def spread(pieces, axis, mask):
+    while mask:
+        for held in list(pieces):
+            pieces[held | mask] = crossed(pieces[held], axis, mask)
+        mask //= 2
+    return pieces
 
 
 def scattered(term, axis):
@@ -320,7 +328,12 @@
     in_all, down_half, full_rows, far_rows, mod_all = head_exchange(
         w_mlp_in, w_mlp_down, state, packed
     )
-    other_half = crossed(down_half, "seq", 1)
+    top = lax.axis_size("seq") // 2
+    down_rows = jnp.zeros((2, top) + down_half.shape[1:], down_half.dtype)
+    for mask, piece in spread({0: down_half}, "seq", top // 2).items():
+        down_rows = lax.dynamic_update_slice(
+            down_rows, piece[:, None], (0, seq_index % top ^ mask, 0, 0)
+        )
     modulation = mod_all[:, :, :mod_width].transpose(1, 0, 2).reshape(REQ, 3 * D)
     final_total = mod_all[0, 0, mod_width : mod_width + channels]
     own_mod = jnp.sum(jnp.where(request_pick[:, None], modulation, 0.0), axis=0)
@@ -345,9 +358,7 @@
         preferred_element_type=jnp.float32,
     )
     mlp_hidden = jax.nn.gelu(mlp_pre, approximate=True).astype(jnp.bfloat16)
-    even = jnp.where(guided_half == 0, down_half, other_half)
-    odd = jnp.where(guided_half == 0, other_half, down_half)
-    down_rows = jnp.stack([even, odd], axis=1).reshape(D, down_half.shape[2])
+    down_rows = down_rows.reshape(D, down_half.shape[2])
     far_term = down_product(mlp_hidden[:TOK_DEV], down_rows)
     mlp_term = down_product(mlp_hidden[TOK_DEV:], down_rows)
     far_update = crossed(scattered(far_term, "tp").astype(jnp.bfloat16), "seq", far_bit)

time: 272 us -> 313 us (1.15)
  local copies, waits for them, and re-layouts: 30.9 us -> 47.7 us
  waiting for transfers between devices: 43.7 us -> 56.9 us
  other arithmetic: 39.1 us -> 46.2 us
  starting transfers between devices: 9.24 us -> 13.6 us
    ppermute x13 -> x15, waiting for transfers between devices: 43.7 us -> 56.9 us  [crossed(): return jax.tree.map(lambda part: lax.ppermute(part, axis, pairs), value)]
    ppermute x13 -> x15, starting transfers between devices: 5.59 us -> 11 us  [crossed(): return jax.tree.map(lambda part: lax.ppermute(part, axis, pairs), value)]
  transfers between devices with their start and end apart: 16 -> 18, of which waited for: 10 -> 11; matrix products, arithmetic and copies ran while one was open for 27% -> 31% of each run, Pallas kernels for 0% -> 0%
where the time goes in v3:
time: 313 us; the launch traced here: 311 us
  Pallas kernels  119 us (38%)
  waiting for transfers between devices  56.9 us (18%)
  local copies, waits for them, and re-layouts  47.7 us (15%)
  other arithmetic  46.2 us (15%)
  matrix products  26.3 us (8%)
  starting transfers between devices  13.6 us (4%)
    pallas_call x1, Pallas kernels, head_exchange(): pl.pallas_call(functools.partial(head_kernel, n), out_shape=(kind((n, dee...  119 us
    ppermute x15, waiting for transfers between devices, crossed(): return jax.tree.map(lambda part: lax.ppermute(part, axis, pairs), value)  56.9 us
    unnamed x43, local copies, waits for them, and re-layouts  20.9 us
    ppermute x15, starting transfers between devices, crossed(): return jax.tree.map(lambda part: lax.ppermute(part, axis, pairs), value)  11 us
    dot_general x1, matrix products, body(): jnp.dot(jnp.concatenate([far_modded, modded], axis=0), in_all.reshape(D,...  6.37 us
  transfers between devices with their start and end apart: 18, of which 11 were waited for; matrix products, arithmetic and copies ran while one was open for 31% of the time, Pallas kernels for 0%

profile of v3, /device:TPU:0, one launch (start us, length us, event | category | flops | bytes accessed | tf_op | source)
XLA Modules:
  0.0 311.0 jit_solution(13663720391972943525)
XLA Ops:
  9.0 118.7 %shard_map.165 = (bf16[8,384,768]{2,1,0:T(8,128)(2,1)S(1)}, bf16[2,384,768]{2,1,0:T(8,128)(2,1)S(1)}, bf16[288,3072]{1,0:T(8,128)(2,1)S(1)}, bf16[288,3072]{1,0:T(8,128)(2,1)S(1)}, f32[8,2,1280]{2,1,0:T(2,128)S(1)}) custom-call(bf16[384,1536]{1,0:T(8,128)(2,1)S(1)} %copy-done.5, bf16[384,1536]{1,0:T(8,128)(2,1)S(1)} %copy-done.6, ...), custom_call_target="tpu_custom_call" | custom-call | tf_op jit(solution)/shard_map/pallas_call | solution.py:193
  129.0 2.2 copy-done.8
  138.0 10.3 %copy.18 = bf16[3072,3,384]{0,2,1:T(8,128)(2,1)} copy(bf16[3072,3,384]{2,0,1:T(8,128)(2,1)} %param.17) | data formatting | bytes 14155776 | tf_op args[3]
  148.3 2.3 fusion.12
  150.6 5.4 %fusion.25 = f32[288,3,3,128]{3,0,2,1:T(8,128)S(1)} fusion(bf16[3,3,128,3072]{3,2,1,0:T(8,128)(2,1)} %bitcast.63, bf16[288,3072]{1,0:T(8,128)(2,1)S(1)} %fusion.12), kind=kOutput, calls=%fused_computation.34 | convolution fusion | flops 2038431744 | bytes 10174464 | tf_op jit(solution)/shard_map/dot_general | solution.py:351
  157.9 2.1 copy.19
  160.0 2.2 squeeze.4
  165.8 2.3 squeeze.5
  175.6 2.3 subtract_convert_fusion
  186.9 2.5 pad_maximum_fusion
  203.0 2.3 fusion.8
  205.3 6.4 %fusion.24 = bf16[576,768]{1,0:T(8,128)(2,1)} fusion(bf16[3072,768]{1,0:T(8,128)(2,1)} %bitcast.60, bf16[288,3072]{1,0:T(8,128)(2,1)S(1)} %copy-done.13, bf16[288,3072]{1,0:T(8,128)(2,1)S(1)} %fusion.8), kind=kOutput, calls=%fused_computation.33 | convolution fusion | flops 2728968192 | bytes 9142272 | tf_op jit(solution)/shard_map/dot_general | solution.py:355
  212.1 2.2 copy-done.9
  214.4 3.5 %fusion.81 = (f32[3,288]{1,0:T(4,128)S(1)}, f32[3,288,576]{2,1,0:T(8,128)}) fusion(pred[576]{0:T(1024)(128)(4,1)S(1)} %copy-done.19, bf16[288,3,128]{0,2,1:T(8,128)(2,1)} %convert_element_type.151, bf16[288,3,128]{2,0,1:T(8,128)(2,1)} %collective-permute-done.1, bf16[288,3,128]{2,0,1:T(8,128)(2,1)} %copy.22), kind=kOutput, calls=%fused_computation.170 | convolution fusion | flops 130277952 | bytes 2658240 | tf_op jit(solution)/shard_map/sub | solution.py:390
  219.3 2.2 fusion.31
  226.7 17.5 %collective-permute-done.4 = bf16[2,384,768]{2,1,0:T(8,128)(2,1)S(1)} collective-permute-done((bf16[2,384,768]{2,1,0:T(8,128)(2,1)}, bf16[2,384,768]{2,1,0:T(8,128)(2,1)S(1)}, u32[]{:S(2)}, u32[]{:S(2)}) %collective-permute-start.4) | collective-permute-done | bytes 1179680 | tf_op jit(solution)/shard_map/ppermute | solution.py:31
  252.0 10.5 %collective-permute-done.10 = bf16[288,768]{1,0:T(8,128)(2,1)S(1)} collective-permute-done((bf16[288,768]{1,0:T(8,128)(2,1)S(1)}, bf16[288,768]{1,0:T(8,128)(2,1)S(1)}, u32[]{:S(2)}, u32[]{:S(2)}) %collective-permute-start.10) | collective-permute-done | bytes 442400 | tf_op jit(solution)/shard_map/ppermute | solution.py:31
  262.9 2.7 collective-permute-start.11
  266.4 2.3 fusion.27
  271.1 12.7 %collective-permute-done.11 = bf16[288,768]{1,0:T(8,128)(2,1)S(1)} collective-permute-done((bf16[288,768]{1,0:T(8,128)(2,1)S(1)}, bf16[288,768]{1,0:T(8,128)(2,1)S(1)}, u32[]{:S(2)}, u32[]{:S(2)}) %collective-permute-start.11) | collective-permute-done | bytes 442400 | tf_op jit(solution)/shard_map/ppermute | solution.py:31
  288.7 5.1 %collective-permute-done.13 = f32[288,128]{0,1:T(8,128)S(1)} collective-permute-done((f32[288,128]{0,1:T(8,128)S(1)}, f32[288,128]{0,1:T(8,128)S(1)}, u32[]{:S(2)}, u32[]{:S(2)}) %collective-permute-start.13) | collective-permute-done | bytes 147488 | tf_op jit(solution)/shard_map/ppermute | solution.py:31
  300.1 3.5 %collective-permute-done.16 = f32[4]{0:T(128)S(1)} collective-permute-done((f32[4]{0:T(128)S(1)}, f32[4]{0:T(128)S(1)}, u32[]{:S(2)}, u32[]{:S(2)}) %collective-permute-start.16) | collective-permute-done | bytes 48 | tf_op jit(solution)/shard_map/ppermute | solution.py:31
  304.9 3.3 %collective-permute-done.17 = f32[4]{0:T(128)S(1)} collective-permute-done((f32[4]{0:T(128)S(1)}, f32[4]{0:T(128)S(1)}, u32[]{:S(2)}, u32[]{:S(2)}) %collective-permute-start.17) | collective-permute-done | bytes 48 | tf_op jit(solution)/shard_map/ppermute | solution.py:31
  308.8 2.3 fusion.59
  (151 shorter events, 82.6 us)
Async XLA Ops:
  0.6 220.8 %copy-start = (bf16[384,3072]{1,0:T(8,128)(2,1)S(1)}, bf16[384,3072]{1,0:T(8,128)(2,1)}, u32[]{:S(2)}) copy-start(bf16[384,3072]{1,0:T(8,128)(2,1)} %param.21) | copy-start | bytes 7077892
  131.2 86.6 %collective-permute-start.2 = (bf16[2,384,768]{2,1,0:T(8,128)(2,1)S(1)}, bf16[2,384,768]{2,1,0:T(8,128)(2,1)}, u32[]{:S(2)}, u32[]{:S(2)}) collective-permute-start(bf16[2,384,768]{2,1,0:T(8,128)(2,1)S(1)} %get-tuple-element.13), channel_id=1, source_target_pairs={{0,8},{4,12},{8,0},{12,4},{16,24},{20,28},{24,16},{28,20},{1,9},{5... | collective-permute-start | bytes 3538952 | tf_op jit(solution)/shard_map/ppermute | solution.py:31
  131.2 94.1 %collective-permute-start.3 = (bf16[2,384,768]{2,1,0:T(8,128)(2,1)S(1)}, bf16[2,384,768]{2,1,0:T(8,128)(2,1)}, u32[]{:S(2)}, u32[]{:S(2)}) collective-permute-start(bf16[2,384,768]{2,1,0:T(8,128)(2,1)S(1)} %get-tuple-element.13), channel_id=1, source_target_pairs={{0,4},{4,0},{8,12},{12,8},{16,20},{20,16},{24,28},{28,24},{1,5},{5... | collective-permute-start | bytes 3538952 | tf_op jit(solution)/shard_map/ppermute | solution.py:31
  183.1 31.2 %collective-permute-start.1 = (bf16[288,3,128]{2,0,1:T(8,128)(2,1)}, bf16[288,3,128]{2,0,1:T(8,128)(2,1)}, u32[]{:S(2)}, u32[]{:S(2)}) collective-permute-start(bf16[288,3,128]{2,0,1:T(8,128)(2,1)} %copy.22), channel_id=1, source_target_pairs={{0,8},{4,12},{8,0},{12,4},{16,24},{20,28},{24,16},{28,20},{1,9},{5... | collective-permute-start | bytes 663560 | tf_op jit(solution)/shard_map/ppermute | solution.py:26
  186.8 32.4 %collective-permute-start = (bf16[288,3,128]{2,0,1:T(8,128)(2,1)}, bf16[288,3,128]{2,0,1:T(8,128)(2,1)}, u32[]{:S(2)}, u32[]{:S(2)}) collective-permute-start(bf16[288,3,128]{2,0,1:T(8,128)(2,1)} %fusion.50), channel_id=1, source_target_pairs={{0,8},{4,12},{8,0},{12,4},{16,24},{20,28},{24,16},{28,20},{1,9},{5... | collective-permute-start | bytes 663560 | tf_op jit(solution)/shard_map/ppermute | solution.py:26
  217.8 26.3 %collective-permute-start.4 = (bf16[2,384,768]{2,1,0:T(8,128)(2,1)}, bf16[2,384,768]{2,1,0:T(8,128)(2,1)S(1)}, u32[]{:S(2)}, u32[]{:S(2)}) collective-permute-start(bf16[2,384,768]{2,1,0:T(8,128)(2,1)} %collective-permute-done.2), channel_id=1, source_target_pairs={{0,4},{4,0},{8,12},{12,8},{16,20},{20,16},{24,28},{28,24},{1,5},{5... | collective-permute-start | bytes 3538952 | tf_op jit(solution)/shard_map/ppermute | solution.py:31
  223.8 20.4 %copy-start.15 = (bf16[576,768]{1,0:T(8,128)(2,1)S(1)}, bf16[576,768]{1,0:T(8,128)(2,1)}, u32[]{:S(2)}) copy-start(bf16[576,768]{1,0:T(8,128)(2,1)} %fusion.24) | copy-start | bytes 2654212
  246.0 3.1 %collective-permute-start.8 = (bf16[288,768]{1,0:T(8,128)(2,1)S(1)}, bf16[288,768]{1,0:T(8,128)(2,1)S(1)}, u32[]{:S(2)}, u32[]{:S(2)}) collective-permute-start(bf16[288,768]{1,0:T(8,128)(2,1)S(1)} %get-tuple-element.32), channel_id=1, source_target_pairs={{0,1},{1,0},{2,3},{3,2},{4,5},{5,4},{6,7},{7,6},{8,9},{9,8},{10,11... | collective-permute-start | bytes 1327112 | tf_op jit(solution)/shard_map/ppermute | solution.py:31
  246.1 3.1 collective-permute-start.9
  248.6 1.9 collective-permute-start.5
  248.7 2.4 collective-permute-start.6
  249.5 13.1 %collective-permute-start.10 = (bf16[288,768]{1,0:T(8,128)(2,1)S(1)}, bf16[288,768]{1,0:T(8,128)(2,1)S(1)}, u32[]{:S(2)}, u32[]{:S(2)}) collective-permute-start(bf16[288,768]{1,0:T(8,128)(2,1)S(1)} %select_convert_fusion), channel_id=1, source_target_pairs={{0,2},{1,3},{2,0},{3,1},{4,6},{5,7},{6,4},{7,5},{8,10},{9,11},{10,... | collective-permute-start | bytes 1327112 | tf_op jit(solution)/shard_map/ppermute | solution.py:31
  251.5 32.4 %copy-start.4 = (bf16[288,768]{1,0:T(8,128)(2,1)S(1)}, bf16[288,768]{1,0:T(8,128)(2,1)}, u32[]{:S(2)}) copy-start(bf16[288,768]{1,0:T(8,128)(2,1)} %state.1) | copy-start | bytes 1327108
  251.5 19.7 %collective-permute-start.7 = (bf16[288,768]{1,0:T(8,128)(2,1)S(1)}, bf16[288,768]{1,0:T(8,128)(2,1)S(1)}, u32[]{:S(2)}, u32[]{:S(2)}) collective-permute-start(bf16[288,768]{1,0:T(8,128)(2,1)S(1)} %select_convert_fusion.3), channel_id=1, source_target_pairs={{0,2},{1,3},{2,0},{3,1},{4,6},{5,7},{6,4},{7,5},{8,10},{9,11},{10,... | collective-permute-start | bytes 1327112 | tf_op jit(solution)/shard_map/ppermute | solution.py:31
  262.9 20.9 %collective-permute-start.11 = (bf16[288,768]{1,0:T(8,128)(2,1)S(1)}, bf16[288,768]{1,0:T(8,128)(2,1)S(1)}, u32[]{:S(2)}, u32[]{:S(2)}) collective-permute-start(bf16[288,768]{1,0:T(8,128)(2,1)S(1)} %add_convert_fusion.1), channel_id=1, source_target_pairs={{0,16},{4,20},{8,24},{12,28},{16,0},{20,4},{24,8},{28,12},{1,17},{... | collective-permute-start | bytes 1327112 | tf_op jit(solution)/shard_map/ppermute | solution.py:31
  268.7 15.8 %copy-start.16 = (bf16[768,64]{0,1:T(8,128)(2,1)S(1)}, bf16[768,64]{0,1:T(8,128)(2,1)}, u32[]{:S(2)}) copy-start(bf16[768,64]{0,1:T(8,128)(2,1)} %param.23) | copy-start | bytes 294916
  269.5 15.5 %copy-start.20 = (s32[2]{0:T(128)S(1)}, s32[2]{0:T(128)}, u32[]{:S(2)}) copy-start(s32[2]{0:T(128)} %param.26) | copy-start | bytes 28
  284.5 26.5 %copy-start.11 = (bf16[288,768]{1,0:T(8,128)(2,1)}, bf16[288,768]{1,0:T(8,128)(2,1)S(1)}, u32[]{:S(2)}) copy-start(bf16[288,768]{1,0:T(8,128)(2,1)S(1)} %get-tuple-element.28) | copy-start | bytes 1327108
  284.9 1.5 collective-permute-start.12
  286.5 7.3 %collective-permute-start.13 = (f32[288,128]{0,1:T(8,128)S(1)}, f32[288,128]{0,1:T(8,128)S(1)}, u32[]{:S(2)}, u32[]{:S(2)}) collective-permute-start(f32[288,128]{0,1:T(8,128)S(1)} %fusion.79), channel_id=1, source_target_pairs={{0,2},{1,3},{2,0},{3,1},{4,6},{5,7},{6,4},{7,5},{8,10},{9,11},{10,... | collective-permute-start | bytes 442376 | tf_op jit(solution)/shard_map/ppermute | solution.py:31
  296.4 3.5 %collective-permute-start.15 = (f32[4]{0:T(128)S(1)}, f32[4]{0:T(128)S(1)}, u32[]{:S(2)}, u32[]{:S(2)}) collective-permute-start(f32[4]{0:T(128)S(1)} %pad_maximum_fusion.3), channel_id=1, source_target_pairs={{0,4},{4,0},{8,12},{12,8},{16,20},{20,16},{24,28},{28,24},{1,5},{5... | collective-permute-start | bytes 56 | tf_op jit(solution)/shard_map/ppermute | solution.py:31
  298.0 10.7 %collective-permute-start.14 = (bf16[144,64]{0,1:T(8,128)(2,1)S(1)}, bf16[144,64]{0,1:T(8,128)(2,1)S(1)}, u32[]{:S(2)}, u32[]{:S(2)}) collective-permute-start(bf16[144,64]{0,1:T(8,128)(2,1)S(1)} %dynamic-slice_convert_fusion), channel_id=1, source_target_pairs={{0,4},{4,0},{8,12},{12,8},{16,20},{20,16},{24,28},{28,24},{1,5},{5... | collective-permute-start | bytes 55304 | tf_op jit(solution)/shard_map/ppermute | solution.py:26
  300.1 3.5 %collective-permute-start.16 = (f32[4]{0:T(128)S(1)}, f32[4]{0:T(128)S(1)}, u32[]{:S(2)}, u32[]{:S(2)}) collective-permute-start(f32[4]{0:T(128)S(1)} %pad_maximum_fusion.4), channel_id=1, source_target_pairs={{0,8},{4,12},{8,0},{12,4},{16,24},{20,28},{24,16},{28,20},{1,9},{5... | collective-permute-start | bytes 56 | tf_op jit(solution)/shard_map/ppermute | solution.py:31
  303.8 4.4 %collective-permute-start.17 = (f32[4]{0:T(128)S(1)}, f32[4]{0:T(128)S(1)}, u32[]{:S(2)}, u32[]{:S(2)}) collective-permute-start(f32[4]{0:T(128)S(1)} %pad_maximum_fusion.5), channel_id=1, source_target_pairs={{0,16},{4,20},{8,24},{12,28},{16,0},{20,4},{24,8},{28,12},{1,17},{... | collective-permute-start | bytes 56 | tf_op jit(solution)/shard_map/ppermute | solution.py:31
  (15 other events, 61.1 us)
